TPU v7x, 32 devices: a whole 2x2x4 slice. The times are simulated.
32 devices in a mesh: groups: 2 (over y), inst: 4 (over x, core), tp: 4 (over z).
Axes of the slice: x: 2, y: 2, z: 4, core: 2. Of those that a mesh axis runs over, the one named last changes fastest.
Arguments:
- hidden_rows: bfloat16 [128, 2, 8192], P(('groups', 'inst')), parts along dimension 0, may hold values from -6 to 6
- queries: bfloat16 [128, 2, 8192], P(('groups', 'inst'), None, 'tp'), parts along dimension 0
- key_pool: bfloat16 [384, 64, 1024], P(('groups', 'inst'), None, 'tp'), parts along dimension 0
- value_pool: bfloat16 [384, 64, 1024], P(('groups', 'inst'), None, 'tp'), parts along dimension 0, may hold values from -6 to 6
- page_table: int32 [128, 4], P(('groups', 'inst')), parts along dimension 0, may hold values from 0 to 47, as said below
- cache_length: int32 [128], P(('groups', 'inst')), parts along dimension 0, may hold values from 1 to 256, as said below
- new_owner: int32 [128, 1], P(('groups', 'inst')), parts along dimension 0, may hold values from 0 to 3; in each aligned block of 16 rows (0 to 15, 16 to 31, ...) at most 6 rows name the same one
- key_weight: bfloat16 [8192, 1024], P(None, 'tp'), may hold values from -0.0625 to 0.0625
- value_weight: bfloat16 [8192, 1024], P(None, 'tp'), may hold values from -0.0625 to 0.0625
Outputs:
- own_out: bfloat16 [128, 2, 8192], P(('groups', 'inst'), None, 'tp'), parts along dimension 0
- adopted_out: bfloat16 [8, 4, 24, 2, 2048], P(('groups', 'inst'), 'tp'), parts along dimension 0
- adopted_pool: bfloat16 [8, 4, 24, 2, 256, 256], P(('groups', 'inst'), 'tp'), parts along dimension 0
There are 2 independent parts, one for each index of `groups`. A program takes and returns all parts, laid end to end along the dimension named above; an argument that names none is the same for every part. Nothing has to cross between parts.
Inputs may be any that keep to these rules, and one draw needn't show every extreme that they name: `page_table`: entries index blocks of the request's own instance pool; only the first ceil(cache_length / 64) entries of a row are read, and no block is read by two requests. `cache_length`: every instance has a request of exactly 256 tokens; each of its other requests needs at most 5/8 of 4 blocks, rounded down, and one of them needs exactly that many. `new_owner`: among the 16 requests of one instance at most 6 name the same instance, a bound that some block reaches of them.
All inputs are finite; a program needn't handle non-finite values.
Results may differ from a plain program's by a relative error of at most 0.0051.
Values may be sent and summed in bfloat16 or wider, within the bound.
No kernel may reach another device: no remote copies, remote signals or barrier semaphores. Data moves between devices by JAX's collectives and lax.ppermute only.
A program may use at most 128 MiB of HBM per device.

v0:
```python
import jax
import jax.numpy as jnp
from jax import lax
from jax.sharding import PartitionSpec as P

HD = 128


ROTARY_BASE = 500000.0


def shifted(value, axis, steps):
    count = lax.axis_size(axis)
    leading, last = (max(0, -steps), min(count, count - steps))
    return lax.ppermute(value, axis, [(source, source + steps) for source in range(leading, last)])


def rotate(values, positions):
    head_width = values.shape[-1]
    half_width = head_width // 2
    frequency = ROTARY_BASE ** (-(jnp.arange(half_width, dtype=jnp.float32) * 2.0 / head_width))
    angles = positions[..., None, None] * frequency
    cosine = jnp.cos(angles)
    sine_part = jnp.sin(angles)
    first_half = values[..., :half_width]
    second_half = values[..., half_width:]
    return jnp.concatenate(
        [
            first_half * cosine - second_half * sine_part,
            second_half * cosine + first_half * sine_part,
        ],
        axis=-1,
    )


def new_tokens(hidden, weight_key, weight_value, lengths):
    count = hidden.shape[0]
    flat_rows = hidden.reshape(count * 2, hidden.shape[-1])
    raw_keys = jnp.dot(flat_rows, weight_key, preferred_element_type=jnp.float32).reshape(
        count, 2, -1, HD
    )
    positions = lengths.astype(jnp.float32)[:, None] + jnp.arange(2, dtype=jnp.float32)[None, :]
    fresh_keys = rotate(raw_keys, positions).reshape(count, 2, -1).astype(jnp.bfloat16)
    fresh_values = (
        jnp.dot(flat_rows, weight_value, preferred_element_type=jnp.float32)
        .reshape(count, 2, -1)
        .astype(jnp.bfloat16)
    )
    return (fresh_keys, fresh_values)


def attend(key_rows, value_rows, lengths, query_rows, fresh_keys, fresh_values):
    count = key_rows.shape[0]
    span_rows = key_rows.shape[1]
    head_groups = key_rows.shape[-1] // HD
    per_group = query_rows.shape[-1] // (head_groups * HD)
    query_heads = query_rows.reshape(count, 2, head_groups, per_group, HD)
    cache_keys = key_rows.reshape(count, span_rows, head_groups, HD)
    cache_values = value_rows.reshape(count, span_rows, head_groups, HD)
    new_keys = fresh_keys.reshape(count, 2, head_groups, HD)
    new_values = fresh_values.reshape(count, 2, head_groups, HD)
    scaling = HD ** (-0.5)
    cache_scores = (
        jnp.einsum("sjgqe,stge->sjgqt", query_heads, cache_keys, preferred_element_type=jnp.float32)
        * scaling
    )
    live_mask = jnp.arange(span_rows)[None, :] < lengths[:, None]
    cache_scores = jnp.where(live_mask[:, None, None, None, :], cache_scores, -jnp.inf)
    fresh_scores = (
        jnp.einsum("sjgqe,sige->sjgqi", query_heads, new_keys, preferred_element_type=jnp.float32)
        * scaling
    )
    allowed = jnp.arange(2)[None, :] <= jnp.arange(2)[:, None]
    fresh_scores = jnp.where(allowed[None, :, None, None, :], fresh_scores, -jnp.inf)
    highest = jnp.maximum(jnp.max(cache_scores, axis=-1), jnp.max(fresh_scores, axis=-1))
    cache_mass = jnp.exp(cache_scores - highest[..., None])
    fresh_mass = jnp.exp(fresh_scores - highest[..., None])
    total_mass = jnp.sum(cache_mass, axis=-1) + jnp.sum(fresh_mass, axis=-1)
    cache_weights = (cache_mass / total_mass[..., None]).astype(jnp.bfloat16)
    fresh_weights = (fresh_mass / total_mass[..., None]).astype(jnp.bfloat16)
    final_output = jnp.einsum(
        "sjgqt,stge->sjgqe", cache_weights, cache_values, preferred_element_type=jnp.float32
    )
    final_output = final_output + jnp.einsum(
        "sjgqi,sige->sjgqe", fresh_weights, new_values, preferred_element_type=jnp.float32
    )
    return final_output.reshape(count, 2, -1).astype(jnp.bfloat16)


def local(
    hidden_rows,
    queries,
    key_pool,
    value_pool,
    page_table,
    cache_length,
    new_owner,
    key_weight,
    value_weight,
):
    halved_count = lax.axis_size("tp") // 2
    remaining_device = lax.axis_index("tp") < halved_count
    instances = lax.axis_size("inst")
    requests = cache_length.shape[0]
    pages_most = page_table.shape[1]
    block_rows = key_pool.shape[1]
    group_width = key_pool.shape[2]
    capacity = max(2, 3 * requests // (2 * instances))
    slot_count = instances * capacity
    span_rows = pages_most * block_rows
    own_keys = key_pool[page_table].reshape(requests, span_rows, group_width)
    own_values = value_pool[page_table].reshape(requests, span_rows, group_width)
    own_fresh_k, own_fresh_v = new_tokens(hidden_rows, key_weight, value_weight, cache_length)
    local_output = attend(own_keys, own_values, cache_length, queries, own_fresh_k, own_fresh_v)
    owner_ids = new_owner[:, 0]
    request_index = jnp.arange(requests)
    same_owner = owner_ids[:, None] == owner_ids[None, :]
    arrival = jnp.sum(same_owner & (request_index[None, :] < request_index[:, None]), axis=1)
    target = owner_ids * capacity + arrival
    chosen = target[None, :] == jnp.arange(slot_count)[:, None]
    picker = chosen.astype(jnp.bfloat16)
    send_pages = jnp.sum(jnp.where(chosen[:, :, None], page_table[None, :, :], 0), axis=1)
    send_len = jnp.sum(jnp.where(chosen, cache_length[None, :], 0), axis=1).reshape(
        instances, capacity
    )

    def pick_rows(rows):
        flat_rows = rows.reshape(requests, -1)
        picked = jnp.dot(picker, flat_rows, preferred_element_type=jnp.float32).astype(jnp.bfloat16)
        return picked.reshape((instances, capacity) + rows.shape[1:])

    fresh_pair = jnp.stack([own_fresh_k, own_fresh_v], axis=2)
    key_rows = key_pool[send_pages].reshape(instances, capacity * span_rows, group_width)
    value_rows = value_pool[send_pages].reshape(instances, capacity * span_rows, group_width)
    sent_blocks = lax.all_to_all(
        jnp.stack([key_rows, value_rows], axis=1), "inst", split_axis=0, concat_axis=0, tiled=True
    )
    sent_queries = lax.all_to_all(
        pick_rows(queries), "inst", split_axis=0, concat_axis=0, tiled=True
    )
    sent_fresh = lax.all_to_all(
        pick_rows(fresh_pair), "inst", split_axis=0, concat_axis=0, tiled=True
    )
    sent_len = lax.all_to_all(send_len, "inst", split_axis=0, concat_axis=0, tiled=True)
    block_count = sent_blocks.size // group_width
    query_count = sent_queries.size // group_width
    packed = jnp.concatenate(
        [
            sent_blocks.reshape(-1, group_width),
            sent_queries.reshape(-1, group_width),
            sent_fresh.reshape(-1, group_width),
        ],
        axis=0,
    )
    moved_rows = shifted(packed, "tp", -halved_count)
    got_len = shifted(sent_len, "tp", -halved_count).reshape(slot_count)
    blocks = moved_rows[:block_count].reshape(sent_blocks.shape)
    got_queries = moved_rows[block_count : block_count + query_count].reshape(slot_count, 2, -1)
    fresh_moved = moved_rows[block_count + query_count :].reshape(slot_count, 2, 2, group_width)
    fresh_k = fresh_moved[:, :, 0]
    fresh_v = fresh_moved[:, :, 1]
    got_keys = blocks[:, 0].reshape(slot_count, span_rows, group_width)
    got_values = blocks[:, 1].reshape(slot_count, span_rows, group_width)
    inherited_requests = attend(got_keys, got_values, got_len, got_queries, fresh_k, fresh_v)
    inherited_requests = jnp.where(
        (got_len > 0)[:, None, None], inherited_requests, jnp.zeros_like(inherited_requests)
    )
    inherited_requests = jnp.where(
        remaining_device, inherited_requests, jnp.zeros_like(inherited_requests)
    )
    token_live = (jnp.arange(span_rows)[None, :] < got_len[:, None])[:, None, :, None]
    kept_cache = jnp.stack([got_keys, got_values], axis=1)
    kept_cache = jnp.where(token_live & remaining_device, kept_cache, jnp.zeros_like(kept_cache))
    local_output = jnp.where(remaining_device, local_output, jnp.zeros_like(local_output))
    return (local_output, inherited_requests[None, None], kept_cache[None, None])


def solution(mesh):
    placed = (
        P(("groups", "inst"), None, None),
        P(("groups", "inst"), None, "tp"),
        P(("groups", "inst"), None, "tp"),
        P(("groups", "inst"), None, "tp"),
        P(("groups", "inst"), None),
        P(("groups", "inst")),
        P(("groups", "inst"), None),
        P(None, "tp"),
        P(None, "tp"),
    )
    return jax.shard_map(
        local,
        mesh=mesh,
        in_specs=placed,
        out_specs=(
            P(("groups", "inst"), None, "tp"),
            P(("groups", "inst"), "tp", None, None, None),
            P(("groups", "inst"), "tp", None, None, None, None),
        ),
        check_vma=False,
    )
```

profile of v0, /device:TPU:0, one launch (start us, length us, event | category | flops | bytes accessed | tf_op | source)
XLA Modules:
  0.0 449.8 jit_solution(11062001169893879079)
XLA Ops:
  0.7 1.0 convert_reduce_fusion
  3.0 6.4 %copy.124 = bf16[256,8192]{1,0:T(8,128)(2,1)} copy(bf16[256,8192]{0,1:T(8,128)(2,1)} %bitcast.91) | data formatting | bytes 8388608 | tf_op jit(solution)/shard_map/dot_general | solution.py:39
  9.4 3.3 fusion.40
  12.9 1.4 fusion.45
  15.9 4.2 all-to-all-start.3
  20.9 0.8 reshape.304
  21.7 2.6 gather_fusion.3
  24.3 2.6 gather_fusion.2
  26.9 3.4 all-to-all-start.2
  30.2 6.1 %pad_maximum_fusion.1 = bf16[4,2,1536,256]{3,2,1,0:T(8,128)(2,1)} fusion(bf16[4,1,1536,256]{3,2,1,0:T(8,128)(2,1)} %bitcast.89, bf16[4,1,1536,256]{3,2,1,0:T(8,128)(2,1)} %bitcast.90), kind=kLoop, calls=%fused_computation.5 | loop fusion | flops 3145728 | bytes 12582912 | tf_op jit(solution)/shard_map/stack | solution.py:136
  36.4 5.2 %all-to-all-start.1 = ((bf16[4,2,1536,256]{3,2,1,0:T(8,128)(2,1)}), bf16[4,2,1536,256]{3,2,1,0:T(8,128)(2,1)}, u32[]{:S(2)}, u32[]{:S(2)}) async-start(bf16[4,2,1536,256]{3,2,1,0:T(8,128)(2,1)} %pad_maximum_fusion.1), calls=%async_computation.1 | async-start | bytes 12582912 | tf_op jit(solution)/shard_map/all_to_all | solution.py:135
  42.4 69.9 %all-to-all-done.1 = bf16[4,2,1536,256]{3,2,1,0:T(8,128)(2,1)} async-done(((bf16[4,2,1536,256]{3,2,1,0:T(8,128)(2,1)}), bf16[4,2,1536,256]{3,2,1,0:T(8,128)(2,1)}, u32[]{:S(2)}, u32[]{:S(2)}) %all-to-all-start.1) | async-done | bytes 6291488 | tf_op jit(solution)/shard_map/all_to_all | solution.py:135
  112.3 16.5 %pad_maximum_fusion = bf16[12768,256]{1,0:T(8,128)(2,1)} fusion(bf16[96,256]{1,0:T(8,128)(2,1)} %reshape.308, bf16[384,256]{1,0:T(8,128)(2,1)S(1)} %reshape.305, bf16[12288,256]{1,0:T(8,128)(2,1)} %bitcast.18), kind=kLoop, calls=%fused_computation.4 | loop fusion | flops 19611648 | bytes 13074432 | tf_op jit(solution)/shard_map/concatenate | solution.py:147
  128.8 1.3 collective-permute-start.1
  130.9 3.4 all-to-all-start
  135.3 2.0 gather_fusion.1
  137.3 2.0 gather_fusion
  139.3 4.0 reshape_reshape.10
  143.3 4.0 reshape_reshape.9
  148.2 2.3 fusion.75
  151.9 1.3 collective-permute-start
  153.9 260.6 %collective-permute-done = s32[4,6]{1,0:T(4,128)S(1)} collective-permute-done((s32[4,6]{1,0:T(4,128)S(1)}, s32[4,6]{1,0:T(4,128)S(1)}, u32[]{:S(2)}, u32[]{:S(2)}) %collective-permute-start) | collective-permute-done | bytes 128 | tf_op jit(solution)/shard_map/ppermute | solution.py:15
  415.8 0.9 slice.49
  416.8 3.6 slice.46
  420.4 3.1 fusion.74
  423.5 5.5 %reshape_reshape_squeeze.7 = bf16[24,256,2,128]{3,2,1,0:T(2,128)(2,1)} reshape(bf16[4,1,1536,256]{3,2,1,0:T(8,128)(2,1)} %get-tuple-element.14) | data formatting | bytes 6291456 | tf_op jit(solution)/shard_map/reshape;reshape;squeeze | solution.py:58
  429.0 1.0 fusion.77
  430.0 2.9 bitcast_reduce_fusion
  433.6 5.5 %reshape_reshape_squeeze.6 = bf16[24,256,2,128]{3,2,1,0:T(2,128)(2,1)} reshape(bf16[4,1,1536,256]{3,2,1,0:T(8,128)(2,1)} %get-tuple-element.15) | data formatting | bytes 6291456 | tf_op jit(solution)/shard_map/reshape;reshape;squeeze | solution.py:59
  439.1 2.5 fusion.4
  442.1 0.9 copy.108
  443.0 6.8 %maximum_select_fusion = bf16[1,1,24,2,256,256]{5,4,3,2,1,0:T(8,128)(2,1)} fusion(bf16[1,1,24,1,256,256]{5,4,3,2,1,0:T(8,128)(2,1)} %bitcast.86, bf16[1,1,24,1,256,256]{5,4,3,2,1,0:T(8,128)(2,1)} %bitcast.85, pred[24,256]{1,0:T(8,128)(4,1)S(1)} %get-tuple-element.20), kind=kLoop, calls=%fused_computation.6 | loop fusion | flops 6291456 | bytes 12589056 | tf_op jit(solution)/shard_map/jit(_where)/select_n | solution.py:173
  (103 shorter events, 11.9 us)
Async XLA Ops:
  0.6 23.6 %copy-start = (bf16[48,64,256]{2,1,0:T(8,128)(2,1)S(1)}, bf16[48,64,256]{2,1,0:T(8,128)(2,1)}, u32[]{:S(2)}) copy-start(bf16[48,64,256]{2,1,0:T(8,128)(2,1)} %param.11) | copy-start | bytes 4718596
  2.3 18.3 %copy-start.14 = (s32[16]{0:T(128)}, s32[16]{0:T(128)S(1)}, u32[]{:S(2)}) copy-start(s32[16]{0:T(128)S(1)} %multiply_add_fusion.1) | copy-start | bytes 196
  3.0 6.4 %copy-start.4 = (bf16[16,2,8192]{2,1,0:T(2,128)(2,1)S(1)}, bf16[16,2,8192]{2,1,0:T(2,128)(2,1)}, u32[]{:S(2)}) copy-start(bf16[16,2,8192]{2,1,0:T(2,128)(2,1)} %param.9) | copy-start | bytes 1572868
  9.3 3.4 copy-start.3
  9.4 3.6 copy-start.5
  12.6 7.6 %copy-start.13 = (s32[16,4]{0,1:T(4,128)S(1)}, s32[16,4]{0,1:T(4,128)}, u32[]{:S(2)}) copy-start(s32[16,4]{0,1:T(4,128)} %param.13) | copy-start | bytes 772
  12.6 7.9 %copy-start.7 = (bf16[16,2,2048]{2,1,0:T(2,128)(2,1)S(1)}, bf16[16,2,2048]{2,1,0:T(2,128)(2,1)}, u32[]{:S(2)}) copy-start(bf16[16,2,2048]{2,1,0:T(2,128)(2,1)} %param.10) | copy-start | bytes 393220
  12.9 8.8 %copy-start.2 = (bf16[48,64,256]{2,1,0:T(8,128)(2,1)S(1)}, bf16[48,64,256]{2,1,0:T(8,128)(2,1)}, u32[]{:S(2)}) copy-start(bf16[48,64,256]{2,1,0:T(8,128)(2,1)} %param.12) | copy-start | bytes 4718596
  14.4 0.6 copy-start.9
  14.4 0.6 copy-start.11
  15.9 10.9 %all-to-all-start.3 = ((bf16[4,6,2,2,256]{4,3,2,1,0:T(2,128)(2,1)}), bf16[4,6,2,2,256]{4,3,2,1,0:T(2,128)(2,1)S(1)}, u32[]{:S(2)}, u32[]{:S(2)}) async-start(bf16[4,6,2,2,256]{4,3,2,1,0:T(2,128)(2,1)} %reshape.307), calls=%async_computation.3 | async-start | bytes 98304 | tf_op jit(solution)/shard_map/all_to_all | solution.py:141
  26.9 9.5 %all-to-all-start.2 = ((bf16[4,6,2,2048]{3,2,1,0:T(2,128)(2,1)}), bf16[4,6,2,2048]{3,2,1,0:T(2,128)(2,1)S(1)}, u32[]{:S(2)}, u32[]{:S(2)}) async-start(bf16[4,6,2,2048]{3,2,1,0:T(2,128)(2,1)} %reshape.304), calls=%async_computation.2 | async-start | bytes 393216 | tf_op jit(solution)/shard_map/all_to_all | solution.py:138
  36.4 76.0 %all-to-all-start.1 = ((bf16[4,2,1536,256]{3,2,1,0:T(8,128)(2,1)}), bf16[4,2,1536,256]{3,2,1,0:T(8,128)(2,1)}, u32[]{:S(2)}, u32[]{:S(2)}) async-start(bf16[4,2,1536,256]{3,2,1,0:T(8,128)(2,1)} %pad_maximum_fusion.1), calls=%async_computation.1 | async-start | bytes 12582912 | tf_op jit(solution)/shard_map/all_to_all | solution.py:135
  112.3 17.8 %copy-start.15 = (s32[16]{0:T(128)S(1)}, s32[16]{0:T(128)}, u32[]{:S(2)}) copy-start(s32[16]{0:T(128)} %copy-done.14) | copy-start | bytes 196
  112.3 17.8 %copy-start.16 = (s32[16]{0:T(128)S(1)}, s32[16]{0:T(128)}, u32[]{:S(2)}) copy-start(s32[16]{0:T(128)} %param.14) | copy-start | bytes 196
  112.3 22.0 %copy-start.8 = (bf16[16,2,2048]{2,1,0:T(2,128)(2,1)S(1)}, bf16[16,2,2048]{2,1,0:T(2,128)(2,1)}, u32[]{:S(2)}) copy-start(bf16[16,2,2048]{2,1,0:T(2,128)(2,1)} %param.10) | copy-start | bytes 393220
  128.8 285.8 %collective-permute-start.1 = (bf16[12768,256]{1,0:T(8,128)(2,1)}, bf16[12768,256]{1,0:T(8,128)(2,1)}, u32[]{:S(2)}, u32[]{:S(2)}) collective-permute-start(bf16[12768,256]{1,0:T(8,128)(2,1)} %pad_maximum_fusion), channel_id=1, source_target_pairs={{2,0},{3,1},{6,4},{7,5},{10,8},{11,9},{14,12},{15,13},{18,16},{19,... | collective-permute-start | bytes 19611656 | tf_op jit(solution)/shard_map/ppermute | solution.py:15
  130.9 21.0 %all-to-all-start = ((s32[4,1,6]{2,1,0:T(1,128)}), s32[4,1,6]{2,1,0:T(1,128)S(1)}, u32[]{:S(2)}, u32[]{:S(2)}) async-start(s32[4,1,6]{2,1,0:T(1,128)} %bitcast.13), calls=%async_computation | async-start | bytes 4096 | tf_op jit(solution)/shard_map/all_to_all | solution.py:144
  143.3 4.0 copy-start.10
  143.3 4.0 copy-start.12
  143.3 4.1 copy-start.17
  147.3 4.0 copy-start.6
  151.9 262.5 %collective-permute-start = (s32[4,6]{1,0:T(4,128)S(1)}, s32[4,6]{1,0:T(4,128)S(1)}, u32[]{:S(2)}, u32[]{:S(2)}) collective-permute-start(s32[4,6]{1,0:T(4,128)S(1)} %bitcast.103), channel_id=1, source_target_pairs={{2,0},{3,1},{6,4},{7,5},{10,8},{11,9},{14,12},{15,13},{18,16},{19,... | collective-permute-start | bytes 296 | tf_op jit(solution)/shard_map/ppermute | solution.py:15
  443.0 6.8 %copy-start.1 = (bf16[48,64,256]{2,1,0:T(8,128)(2,1)S(1)}, bf16[48,64,256]{2,1,0:T(8,128)(2,1)}, u32[]{:S(2)}) copy-start(bf16[48,64,256]{2,1,0:T(8,128)(2,1)} %param.11) | copy-start | bytes 4718596
where the time goes:
time: 451 us; the launch traced here: 450 us
  waiting for transfers between devices  330 us (73%)
  local copies, waits for them, and re-layouts  49.2 us (11%)
  other arithmetic  34.5 us (8%)
  starting transfers between devices  18.8 us (4%)
  matrix products  15.7 us (3%)
    ppermute x2, waiting for transfers between devices, shifted(): lax.ppermute(value, axis, [(source, source + steps) for source in range(l...  261 us
    all_to_all x1, waiting for transfers between devices, local(): lax.all_to_all(jnp.stack([key_rows, value_rows], axis=1), 'inst', split_a...  69.9 us
    concatenate x1, other arithmetic, local(): jnp.concatenate([sent_blocks.reshape(-1, group_width), sent_queries.resha...  16.5 us
    another operation x2, local copies, waits for them, and re-layouts, attend(): cache_keys = key_rows.reshape(count, span_rows, head_groups, HD)  9.52 us
    another operation x2, local copies, waits for them, and re-layouts, attend(): cache_values = value_rows.reshape(count, span_rows, head_groups, HD)  9.49 us
  transfers between devices with their start and end apart: 6, of which 2 were waited for; matrix products, arithmetic and copies ran while one was open for 7% of the time, Pallas kernels for 0%

commit v1 on v0

v1 whole, which is shorter than its diff:
```python
import functools

import jax
import jax.numpy as jnp
from jax import lax
from jax.experimental import pallas as pl
from jax.experimental.pallas import tpu as pltpu
from jax.sharding import PartitionSpec as P

HD = 128
ROTARY_BASE = 500000.0
UNIT = 16
FIRST, STEP = 18, 2
ANY = pl.BlockSpec(memory_space=pl.ANY)
HBM = pl.BlockSpec(memory_space=pltpu.HBM)
VMEM_LIMIT = 60 * 1024 * 1024


def rotate(values, positions):
    head_width = values.shape[-1]
    half_width = head_width // 2
    frequency = ROTARY_BASE ** (-(jnp.arange(half_width, dtype=jnp.float32) * 2.0 / head_width))
    angles = positions[..., None, None] * frequency
    cosine = jnp.cos(angles)
    sine_part = jnp.sin(angles)
    first_half = values[..., :half_width]
    second_half = values[..., half_width:]
    return jnp.concatenate(
        [
            first_half * cosine - second_half * sine_part,
            second_half * cosine + first_half * sine_part,
        ],
        axis=-1,
    )


def new_tokens(hidden, weight_key, weight_value, lengths):
    count = hidden.shape[0]
    flat_rows = hidden.reshape(count * 2, hidden.shape[-1])
    raw_keys = lax.optimization_barrier(
        jnp.dot(flat_rows, weight_key, preferred_element_type=jnp.float32)
    ).reshape(count, 2, -1, HD)
    positions = lengths.astype(jnp.float32)[:, None] + jnp.arange(2, dtype=jnp.float32)[None, :]
    fresh_keys = rotate(raw_keys, positions).reshape(count, 2, -1).astype(jnp.bfloat16)
    fresh_values = (
        jnp.dot(flat_rows, weight_value, preferred_element_type=jnp.float32)
        .reshape(count, 2, -1)
        .astype(jnp.bfloat16)
    )
    return (fresh_keys, fresh_values)


def attend(key_rows, value_rows, lengths, query_rows, fresh_keys, fresh_values):
    count = key_rows.shape[0]
    span_rows = key_rows.shape[1]
    head_groups = key_rows.shape[-1] // HD
    per_group = query_rows.shape[-1] // (head_groups * HD)
    query_heads = query_rows.reshape(count, 2, head_groups, per_group, HD)
    cache_keys = key_rows.reshape(count, span_rows, head_groups, HD)
    cache_values = value_rows.reshape(count, span_rows, head_groups, HD)
    new_keys = fresh_keys.reshape(count, 2, head_groups, HD)
    new_values = fresh_values.reshape(count, 2, head_groups, HD)
    scaling = HD ** (-0.5)
    cache_scores = (
        jnp.einsum("sjgqe,stge->sjgqt", query_heads, cache_keys, preferred_element_type=jnp.float32)
        * scaling
    )
    live_mask = jnp.arange(span_rows)[None, :] < lengths[:, None]
    cache_scores = jnp.where(live_mask[:, None, None, None, :], cache_scores, -jnp.inf)
    fresh_scores = (
        jnp.einsum("sjgqe,sige->sjgqi", query_heads, new_keys, preferred_element_type=jnp.float32)
        * scaling
    )
    allowed = jnp.arange(2)[None, :] <= jnp.arange(2)[:, None]
    fresh_scores = jnp.where(allowed[None, :, None, None, :], fresh_scores, -jnp.inf)
    highest = jnp.maximum(jnp.max(cache_scores, axis=-1), jnp.max(fresh_scores, axis=-1))
    cache_mass = jnp.exp(cache_scores - highest[..., None])
    fresh_mass = jnp.exp(fresh_scores - highest[..., None])
    total_mass = jnp.sum(cache_mass, axis=-1) + jnp.sum(fresh_mass, axis=-1)
    cache_weights = (cache_mass / total_mass[..., None]).astype(jnp.bfloat16)
    fresh_weights = (fresh_mass / total_mass[..., None]).astype(jnp.bfloat16)
    final_output = jnp.einsum(
        "sjgqt,stge->sjgqe", cache_weights, cache_values, preferred_element_type=jnp.float32
    )
    final_output = final_output + jnp.einsum(
        "sjgqi,sige->sjgqe", fresh_weights, new_values, preferred_element_type=jnp.float32
    )
    return final_output.reshape(count, 2, -1).astype(jnp.bfloat16)


def padded(lengths):
    return (lengths + (UNIT - 1)) // UNIT * UNIT


def strides(count):
    bits = []
    step = count // 2
    while step:
        bits.append(step)
        step //= 2
    return bits


def nearness(apart, steps):
    return sum((apart < step).astype(jnp.int32) for step in steps)


def pack_kernel(cuts, steps, table, lens, owners, keys, values, *refs):
    parts = refs[: len(cuts)]
    pools, pile, arrived, left_sems = refs[len(cuts) :]
    count, pages_most = lens.shape[0], table.shape[0]
    block = keys.shape[1]
    row = lax.broadcasted_iota(jnp.int32, (UNIT, keys.shape[2]), 0)
    me = lax.axis_index("inst")
    loads = [
        pltpu.make_async_copy(pool, pools.at[index], arrived.at[index])
        for index, pool in enumerate((keys, values))
    ]
    for load in loads:
        load.start()
    for load in loads:
        load.wait()

    def turn(i, start):
        r = lax.rem(i, count)
        live = lens[r]
        here = nearness(jnp.bitwise_xor(owners[r], me), steps) == i // count

        @pl.when(here)
        def _():
            for page in range(pages_most):

                @pl.when(live > page * block)
                def _():
                    source = table[page, r]
                    place = pl.ds(pl.multiple_of(start + page * block, UNIT), block)
                    for index in range(2):
                        pile[index, place, :] = pools[index, source]

            ending = padded(live) - UNIT
            place = pl.ds(pl.multiple_of(start + ending, UNIT), UNIT)
            mask = row < live - ending
            for index in range(2):
                kept = pile[index, place, :]
                pile[index, place, :] = jnp.where(mask, kept, jnp.zeros_like(kept))

        return start + jnp.where(here, padded(live), 0)

    lax.fori_loop(0, count * (len(steps) + 1), turn, jnp.int32(0))
    leaving = [
        pltpu.make_async_copy(
            pile.at[:, pl.ds(low, high - low), :], parts[number], left_sems.at[number]
        )
        for number, (low, high) in enumerate(cuts)
    ]
    for copy in leaving:
        copy.start()
    for copy in leaving:
        copy.wait()


def pack(page_table, lengths, owners, key_pool, value_pool, cuts, steps):
    width = key_pool.shape[2]
    block = key_pool.shape[1]
    return pl.pallas_call(
        functools.partial(pack_kernel, cuts, steps),
        out_shape=tuple(
            jax.ShapeDtypeStruct((2, high - low, width), jnp.bfloat16) for low, high in cuts
        ),
        grid_spec=pltpu.PrefetchScalarGridSpec(
            num_scalar_prefetch=3,
            grid=(),
            in_specs=[HBM, HBM],
            out_specs=[HBM] * len(cuts),
            scratch_shapes=[
                pltpu.VMEM((2,) + key_pool.shape, jnp.bfloat16),
                pltpu.VMEM((2, cuts[-1][1] + block, width), jnp.bfloat16),
                pltpu.SemaphoreType.DMA((2,)),
                pltpu.SemaphoreType.DMA((len(cuts),)),
            ],
        ),
        compiler_params=pltpu.CompilerParams(vmem_limit_bytes=VMEM_LIMIT),
        name="pack",
    )(page_table.T, lengths, owners, key_pool, value_pool)


def prepare_kernel(count, pile, *refs):
    parts, pool = refs[:count], refs[count]
    held, blank, arrived, sems, pool_sems = refs[count + 1 :]
    load = pltpu.make_async_copy(pile, held, arrived)
    load.start()
    blank[...] = jnp.zeros_like(blank)
    copies = [
        pltpu.make_async_copy(blank, pool.at[slot], pool_sems.at[slot])
        for slot in range(pool.shape[0])
    ]
    for copy in copies:
        copy.start()
    load.wait()
    copies += [
        pltpu.make_async_copy(held.at[:, pl.ds(0, part.shape[1]), :], part, sems.at[number])
        for number, part in enumerate(parts)
    ]
    for copy in copies[pool.shape[0] :]:
        copy.start()
    for copy in copies:
        copy.wait()


def prepare(pile, sizes, pool_shape):
    *parts, pool = pl.pallas_call(
        functools.partial(prepare_kernel, len(sizes)),
        out_shape=[
            jax.ShapeDtypeStruct((2, size, pile.shape[2]), pile.dtype) for size in sizes
        ]
        + [jax.ShapeDtypeStruct(pool_shape, pile.dtype)],
        in_specs=[HBM],
        out_specs=[HBM] * (len(sizes) + 1),
        scratch_shapes=[
            pltpu.VMEM(pile.shape, pile.dtype),
            pltpu.VMEM(pool_shape[1:], pile.dtype),
            pltpu.SemaphoreType.DMA,
            pltpu.SemaphoreType.DMA((len(sizes),)),
            pltpu.SemaphoreType.DMA((pool_shape[0],)),
        ],
        compiler_params=pltpu.CompilerParams(vmem_limit_bytes=VMEM_LIMIT),
        name="prepare",
    )(pile)
    return parts, pool


def entry(plan, count, capacity, kind, j, c):
    return plan[count + (kind * count + j) * capacity + c]


def unpack_kernel(low, high, total, capacity, numbers, plan, *refs):
    count = len(numbers)
    piles, out, stage, inward, outward = refs[:count], refs[-4], refs[-3], refs[-2], refs[-1]

    def span(j, c):
        start = entry(plan, total, capacity, 0, j, c)
        begin = jnp.maximum(start, low)
        end = jnp.minimum(start + entry(plan, total, capacity, 1, j, c), high)
        return start, begin, end - begin

    def arriving(k, c):
        _, begin, rows = span(numbers[k], c)
        rows = pl.multiple_of(rows, UNIT)
        return pltpu.make_async_copy(
            piles[k].at[:, pl.ds(pl.multiple_of(begin - low, UNIT), rows), :],
            stage.at[k * capacity + c, :, pl.ds(0, rows), :],
            inward.at[k * capacity + c],
        )

    def leaving(k, c):
        start, begin, rows = span(numbers[k], c)
        rows = pl.multiple_of(rows, UNIT)
        return pltpu.make_async_copy(
            stage.at[k * capacity + c, :, pl.ds(0, rows), :],
            out.at[
                plan[numbers[k]] * capacity + c,
                :,
                pl.ds(pl.multiple_of(begin - start, UNIT), rows),
                :,
            ],
            outward.at[k * capacity + c],
        )

    def each(action):
        for k in range(count):

            def slot(c, carry):
                @pl.when(span(numbers[k], c)[2] > 0)
                def _():
                    action(k, c)

                return carry

            lax.fori_loop(0, capacity, slot, 0)

    def turn(k, c):
        arriving(k, c).wait()
        leaving(k, c).start()

    each(lambda k, c: arriving(k, c).start())
    each(turn)
    each(lambda k, c: leaving(k, c).wait())


def unpack(plan, total, capacity, parts, out, low, high):
    count = len(parts)
    numbers = [number for _, number in parts]
    return pl.pallas_call(
        functools.partial(unpack_kernel, low, high, total, capacity, numbers),
        out_shape=jax.ShapeDtypeStruct(out.shape, out.dtype),
        grid_spec=pltpu.PrefetchScalarGridSpec(
            num_scalar_prefetch=1,
            grid=(),
            in_specs=[ANY] * count + [HBM],
            out_specs=HBM,
            scratch_shapes=[
                pltpu.VMEM((count * capacity,) + out.shape[1:], out.dtype),
                pltpu.SemaphoreType.DMA((count * capacity,)),
                pltpu.SemaphoreType.DMA((count * capacity,)),
            ],
        ),
        input_output_aliases={1 + count: 0},
        compiler_params=pltpu.CompilerParams(vmem_limit_bytes=VMEM_LIMIT),
        name="unpack",
    )(plan, *[pile for pile, _ in parts], out)


def place_kernel(total, capacity, numbers, plan, *refs):
    out = refs[-1]
    out[...] = jnp.zeros_like(out)
    for k, j in enumerate(numbers):

        def slot(c, carry):
            r = entry(plan, total, capacity, 2, j, c)

            @pl.when(r >= 0)
            def _():
                out[plan[j] * capacity + c] = refs[k][r]

            return carry

        lax.fori_loop(0, capacity, slot, 0)


def place(plan, total, capacity, parts):
    source = parts[0][0].shape
    shape = (total * capacity,) + source[1:]
    return pl.pallas_call(
        functools.partial(place_kernel, total, capacity, [number for _, number in parts]),
        out_shape=jax.ShapeDtypeStruct(shape, jnp.bfloat16),
        grid_spec=pltpu.PrefetchScalarGridSpec(
            num_scalar_prefetch=1,
            grid=(1,),
            in_specs=[pl.BlockSpec(source, lambda i, *_: (0, 0, 0))] * len(parts),
            out_specs=pl.BlockSpec(shape, lambda i, *_: (0, 0, 0)),
        ),
        compiler_params=pltpu.CompilerParams(vmem_limit_bytes=VMEM_LIMIT),
        name="place",
    )(plan, *[part for part, _ in parts])


def local(
    hidden_rows,
    queries,
    key_pool,
    value_pool,
    page_table,
    cache_length,
    new_owner,
    key_weight,
    value_weight,
):
    tp = lax.axis_size("tp")
    halved_count = tp // 2
    remaining_device = lax.axis_index("tp") < halved_count
    instances = lax.axis_size("inst")
    groups = lax.axis_size("groups")
    me = lax.axis_index("inst")
    requests = cache_length.shape[0]
    pages_most = page_table.shape[1]
    block_rows = key_pool.shape[1]
    group_width = key_pool.shape[2]
    capacity = max(2, 3 * requests // (2 * instances))
    slot_count = instances * capacity
    span_rows = pages_most * block_rows
    most = span_rows + (requests - 1) * (pages_most * 5 // 8) * block_rows
    step = STEP * block_rows
    cut = min(most, FIRST * block_rows)
    all_steps = strides(instances)
    order = [0]
    for stride in all_steps:
        order = order + [o ^ stride for o in order]

    def down(value):
        return lax.ppermute(value, "tp", [(t + halved_count, t) for t in range(halved_count)])

    def across(value, stride, low):
        pairs = [
            (i * tp + t, (i ^ stride) * tp + t)
            for i in range(instances)
            for t in range(low, low + halved_count)
        ]
        return lax.ppermute(value, ("inst", "tp"), pairs)

    def spread(value, steps, low=0):
        parts = [(value, 0)]
        for stride in steps:
            parts = parts + [(across(part, stride, low), o ^ stride) for part, o in parts]
        return [(part, order.index(o)) for part, o in parts]

    first, rest = pack(
        page_table,
        cache_length,
        new_owner[:, 0],
        key_pool,
        value_pool,
        [(0, cut), (cut, most)],
        all_steps,
    )
    sample = down(first[:1, :UNIT, :HD])
    first = down(first)
    _, rest, hidden_rows, lengths, new_owner, page_table = lax.optimization_barrier(
        (sample, rest, hidden_rows, cache_length, new_owner, page_table)
    )
    own_keys = key_pool[page_table].reshape(requests, span_rows, group_width)
    own_values = value_pool[page_table].reshape(requests, span_rows, group_width)
    own_fresh_k, own_fresh_v = new_tokens(hidden_rows, key_weight, value_weight, lengths)

    facts = jnp.stack([lengths, new_owner[:, 0]])[None]
    for stride in all_steps:
        facts = jnp.concatenate(
            [facts, lax.ppermute(facts, "inst", [(i, i ^ stride) for i in range(instances)])]
        )
    sources = me ^ jnp.array(order, jnp.int32)
    sizes_all = padded(facts[:, 0])
    near = nearness(facts[:, 1] ^ sources[:, None], all_steps)
    extents = jnp.stack(
        [
            jnp.max(jnp.sum(sizes_all, axis=1)),
            jnp.max(jnp.sum(jnp.where(near == 0, sizes_all, 0), axis=1)),
        ]
    )
    for stride in strides(groups):
        extents = jnp.maximum(
            extents,
            lax.ppermute(extents, "groups", [(g, g ^ stride) for g in range(groups)]),
        )
    mine = facts[:, 1] == me
    index = jnp.arange(requests)
    earlier = index[None, :] < index[:, None]
    packed_earlier = (near[:, None, :] < near[:, :, None]) | (
        (near[:, None, :] == near[:, :, None]) & earlier[None]
    )
    starts_all = jnp.sum(jnp.where(packed_earlier, sizes_all[:, None, :], 0), axis=2)
    rank = jnp.sum(jnp.where(earlier[None], mine[:, None, :].astype(jnp.int32), 0), axis=2)
    chosen = mine[:, None, :] & (rank[:, None, :] == jnp.arange(capacity)[None, :, None])

    def chosen_of(values):
        return jnp.sum(jnp.where(chosen, values, 0), axis=2).reshape(-1)

    plan = jnp.concatenate(
        [
            sources,
            chosen_of(starts_all[:, None, :]),
            jnp.where(remaining_device, chosen_of(sizes_all[:, None, :]), 0),
            chosen_of(index[None, None, :] + 1) - 1,
        ]
    )
    plan_shape = (instances, capacity)

    local_output = attend(own_keys, own_values, cache_length, queries, own_fresh_k, own_fresh_v)
    near_sizes = list(range(step, most - cut, step)) + [most - cut]
    far_sizes = list(range(4 * step, most - cut, 4 * step)) + [most - cut]
    rests, pool = prepare(rest, near_sizes, (slot_count, 2, span_rows, group_width))
    local_output, pool, rests, extents, plan = lax.optimization_barrier(
        (local_output, pool, rests, extents, plan)
    )
    inherited = place(plan, *plan_shape, spread(local_output, all_steps, halved_count))
    first, inherited = lax.optimization_barrier((first, inherited))
    inherited = down(inherited)
    far_first = across(first, all_steps[0], 0)

    def finish(more, far, rests, first, plan, pool):
        if more:
            piece = down(rests[near_sizes.index(more)])
        near_first = [part for part, _ in spread(first, all_steps[1:])[1:]]
        if more:
            pieces = spread(piece, all_steps if far else all_steps[1:])
            pool = unpack(plan, *plan_shape, pieces, pool, cut, cut + more)
        return pool, near_first

    branches = [functools.partial(finish, more, False) for more in [0] + near_sizes]
    branches += [functools.partial(finish, more, True) for more in far_sizes]
    extra = jnp.maximum(extents[0] - cut, 0)
    near_choice = jnp.minimum((extra + step - 1) // step, len(near_sizes))
    far_choice = jnp.clip((extra + 4 * step - 1) // (4 * step) - 1, 0, len(far_sizes) - 1)
    choice = jnp.where(extents[1] > cut, 1 + len(near_sizes) + far_choice, near_choice)
    pool, near_first = lax.switch(choice, branches, rests, first, plan, pool)
    far_first, pool, inherited = lax.optimization_barrier((far_first, pool, inherited))
    places = [0]
    for stride in all_steps[1:]:
        places = places + [o ^ stride for o in places]
    near_parts = [(part, order.index(o)) for part, o in zip([first] + near_first, places)]
    far_parts = [
        (part, order.index(order[number] ^ all_steps[0]))
        for part, number in spread(far_first, all_steps[1:])
    ]
    kept_cache = unpack(plan, *plan_shape, near_parts + far_parts, pool, 0, cut)
    local_output = jnp.where(remaining_device, local_output, jnp.zeros_like(local_output))
    return (local_output, inherited[None, None], kept_cache[None, None])


def solution(mesh):
    placed = (
        P(("groups", "inst"), None, None),
        P(("groups", "inst"), None, "tp"),
        P(("groups", "inst"), None, "tp"),
        P(("groups", "inst"), None, "tp"),
        P(("groups", "inst"), None),
        P(("groups", "inst")),
        P(("groups", "inst"), None),
        P(None, "tp"),
        P(None, "tp"),
    )
    return jax.shard_map(
        local,
        mesh=mesh,
        in_specs=placed,
        out_specs=(
            P(("groups", "inst"), None, "tp"),
            P(("groups", "inst"), "tp", None, None, None),
            P(("groups", "inst"), "tp", None, None, None, None),
        ),
        check_vma=False,
    )
```

time: 451 us -> 112 us (0.25)
  waiting for transfers between devices: 330 us -> 38.2 us
  local copies, waits for them, and re-layouts: 49.2 us -> 14.7 us
  other arithmetic: 34.5 us -> 6.8 us
  Pallas kernels: 0 us -> 18.3 us
    ppermute x2 -> x13, waiting for transfers between devices: 261 us -> 38.2 us  [the longest x3 32.6 us: down(): lax.ppermute(value, 'tp', [(t + halved_count, t) for t in range(halved_co...]
    all_to_all x4 -> x0, waiting for transfers between devices: 69.9 us -> none  [the longest x1 69.9 us: local(): lax.all_to_all(jnp.stack([key_rows, value_rows], axis=1), 'inst', split_a...]
    pallas_call x0 -> x5, Pallas kernels: none -> 18.3 us  [the longest x1 5.82 us: pack(): pl.pallas_call(functools.partial(pack_kernel, cuts, steps), out_shape=tup...]
    concatenate x1 -> x3, other arithmetic: 16.5 us -> 0.1 us  [the longest x1 0.08 us: local(): jnp.concatenate([sources, chosen_of(starts_all[:, None, :]), jnp.where(re...]
    all_to_all x4 -> x0, starting transfers between devices: 16.2 us -> none  [the longest x1 5.24 us: local(): lax.all_to_all(jnp.stack([key_rows, value_rows], axis=1), 'inst', split_a...]
    ppermute x2 -> x13, starting transfers between devices: 2.57 us -> 18.6 us  [the longest x7 10.1 us: across(): return lax.ppermute(value, ('inst', 'tp'), pairs)]
    slice x5 -> x2, local copies, waits for them, and re-layouts: 8.65 us -> 0.75 us  [the longest x1 0.66 us: local(): extra = jnp.maximum(extents[0] - cut, 0)]
    another operation x2 -> x1, local copies, waits for them, and re-layouts: 9.52 us -> 2.03 us  [attend(): cache_keys = key_rows.reshape(count, span_rows, head_groups, HD)]
  transfers between devices with their start and end apart: 6 -> 13, of which waited for: 2 -> 5; matrix products, arithmetic and copies ran while one was open for 7% -> 26% of each run, Pallas kernels for 0% -> 8%
where the time goes in v1:
time: 112 us; the launch traced here: 111 us
  waiting for transfers between devices  38.2 us (34%)
  starting transfers between devices  18.6 us (17%)
  Pallas kernels  18.3 us (16%)
  local copies, waits for them, and re-layouts  14.7 us (13%)
  matrix products  11.8 us (11%)
  other arithmetic  6.8 us (6%)
  between operations  2.47 us (2%)
    ppermute x3, waiting for transfers between devices, down(): lax.ppermute(value, 'tp', [(t + halved_count, t) for t in range(halved_co...  32.6 us
    ppermute x7, starting transfers between devices, across(): return lax.ppermute(value, ('inst', 'tp'), pairs)  10.1 us
    pallas_call x1, Pallas kernels, pack(): pl.pallas_call(functools.partial(pack_kernel, cuts, steps), out_shape=tup...  5.82 us
    pallas_call x2, Pallas kernels, unpack(): pl.pallas_call(functools.partial(unpack_kernel, low, high, total, capacit...  5.48 us
    pallas_call x1, Pallas kernels, prepare(): pl.pallas_call(functools.partial(prepare_kernel, len(sizes)), out_shape=[...  4.31 us
    unnamed x35, local copies, waits for them, and re-layouts  4.06 us
    ppermute x3, starting transfers between devices, down(): lax.ppermute(value, 'tp', [(t + halved_count, t) for t in range(halved_co...  3.86 us
    ppermute x7, waiting for transfers between devices, across(): return lax.ppermute(value, ('inst', 'tp'), pairs)  3.67 us
  transfers between devices with their start and end apart: 13, of which 5 were waited for; matrix products, arithmetic and copies ran while one was open for 26% of the time, Pallas kernels for 8%

profile of v1, /device:TPU:0, one launch (start us, length us, event | category | flops | bytes accessed | tf_op | source)
XLA Modules:
  0.0 111.0 jit_solution(3516921541108741535)
XLA Ops:
  0.7 5.8 %pack.1 = (bf16[2,1152,256]{2,1,0:T(8,128)(2,1)}, bf16[2,1024,256]{2,1,0:T(8,128)(2,1)}) custom-call(s32[4,16]{1,0:T(4,128)} %bitcast.80, s32[16]{0:T(128)} %lens.1, s32[16]{0:T(128)} %bitcast.82, bf16[48,64,256]{2,1,0:T(8,128)(2,1)} %keys.1, bf16[48,64,256]{2,1,0:T(8,128)(2,1)} %values.1), custom_call_target="tpu_custom_call" | custom-call | tf_op jit(solution)/shard_map/pack/pallas_call | solution.py:165
  6.5 3.0 %collective-permute-start.35 = (s32[1,2,16]{2,0,1:T(1,128)S(1)}, s32[1,2,16]{2,0,1:T(1,128)S(1)}, u32[]{:S(2)}, u32[]{:S(2)}) collective-permute-start(s32[1,2,16]{2,0,1:T(1,128)S(1)} %bitcast.77), channel_id=1, source_target_pairs={{0,8},{4,12},{8,0},{12,4},{1,9},{5,13},{9,1},{13,5},{2,10},{6,14},... | collective-permute-start | bytes 392 | tf_op jit(solution)/shard_map/ppermute | solution.py:417
  9.6 1.3 %collective-permute-start.38 = (bf16[2,1152,256]{2,1,0:T(8,128)(2,1)}, bf16[2,1152,256]{2,1,0:T(8,128)(2,1)}, u32[]{:S(2)}, u32[]{:S(2)}) collective-permute-start(bf16[2,1152,256]{2,1,0:T(8,128)(2,1)} %get-tuple-element.180), channel_id=1, source_target_pairs={{2,0},{3,1},{6,4},{7,5},{10,8},{11,9},{14,12},{15,13},{18,16},{19,... | collective-permute-start | bytes 3538952 | tf_op jit(solution)/shard_map/ppermute | solution.py:380
  11.2 2.0 %gather_fusion.1 = bf16[64,64,256]{2,1,0:T(8,128)(2,1)} fusion(bf16[48,64,256]{2,1,0:T(8,128)(2,1)S(1)} %copy-done, s32[1024]{0:T(1024)S(1)} %pad_clamp_fusion), kind=kCustom, calls=%fused_computation.1 | custom fusion | bytes 4194560 | tf_op jit(solution)/shard_map/gather | solution.py:410
  13.2 2.0 %gather_fusion = bf16[64,64,256]{2,1,0:T(8,128)(2,1)} fusion(bf16[48,64,256]{2,1,0:T(8,128)(2,1)S(1)} %copy-done.1, s32[1024]{0:T(1024)S(1)} %pad_clamp_fusion), kind=kCustom, calls=%fused_computation | custom fusion | bytes 4194560 | tf_op jit(solution)/shard_map/gather | solution.py:411
  15.6 3.1 %fusion.26 = bf16[16,2,256]{2,0,1:T(8,128)(2,1)S(1)} fusion(bf16[8192,256]{1,0:T(8,128)(2,1)} %param.29, bf16[16,2,8192]{2,1,0:T(2,128)(2,1)S(1)} %copy-done.4), kind=kOutput, calls=%fused_computation.17 | convolution fusion | flops 134225920 | bytes 4734976 | tf_op jit(solution)/shard_map/dot_general | solution.py:46
  18.7 3.2 %fusion.58 = f32[32,256]{1,0:T(8,128)S(1)} fusion(bf16[32,8192]{1,0:T(8,128)(2,1)S(1)} %reshape.172, bf16[8192,256]{1,0:T(8,128)(2,1)} %param.28), kind=kOutput, calls=%fused_computation.96 | convolution fusion | flops 134217728 | bytes 4751360 | tf_op jit(solution)/shard_map/dot_general | solution.py:41
  22.0 2.0 %reshape_reshape.7 = bf16[16,256,2,128]{3,2,1,0:T(2,128)(2,1)} reshape(bf16[64,64,256]{2,1,0:T(8,128)(2,1)S(1)} %copy-done.3) | data formatting | bytes 4194304 | tf_op jit(solution)/shard_map/reshape;reshape | solution.py:59
  24.4 2.5 %fusion.56 = (f32[16,2,2,8]{3,1,2,0:T(2,128)S(1)}, f32[16,2,2,8,256]{4,3,1,2,0:T(8,128)S(1)}) fusion(bf16[16,2,2,8,128]{4,3,2,1,0:T(8,128)(2,1)S(1)} %reshape.171, bf16[16,256,2,128,1]{3,2,1,0,4:T(2,128)(2,1)} %bitcast.75, pred[16,256]{1,0:T(8,128)(4,1)S(1)} %iota_compare_fusion), kind=kOutput, calls=%fused_computation.94 | convolution fusion | flops 33947136 | bytes 2758656 | tf_op jit(solution)/shard_map/sjgqe,stge->sjgqt/dot_general | solution.py:65
  28.2 2.0 %reshape_reshape.6 = bf16[16,256,2,128]{3,2,1,0:T(2,128)(2,1)} reshape(bf16[64,64,256]{2,1,0:T(8,128)(2,1)S(1)} %copy-done.2) | data formatting | bytes 4194304 | tf_op jit(solution)/shard_map/reshape;reshape | solution.py:60
  30.5 2.0 %fusion.21 = bf16[16,2,2,8,128]{4,3,1,2,0:T(8,128)(2,1)S(1)} fusion(f32[16,2,128,2,8]{2,4,3,1,0:T(8,128)S(1)} %fusion.36, bf16[16,256,2,128,1]{3,2,1,0,4:T(2,128)(2,1)} %bitcast.74, f32[16,2,2,8,256]{4,3,1,2,0:T(8,128)S(1)} %get-tuple-element.220, f32[16,2,2,8]{3,1,2,0:T(2,128)S(1)} %add.89, f32[16,2,2,8]{3,1,2,0:T(2,128)S(1)} %max.18), kind=kOutput, calls=%fused_computation.13 | convolution fusion | flops 34078720 | bytes 3018752 | tf_op jit(solution)/shard_map/sjgqt,stge->sjgqe/dot_general | solution.py:82
  32.7 4.3 %prepare.1 = (bf16[2,128,256]{2,1,0:T(8,128)(2,1)S(1)}, bf16[2,256,256]{2,1,0:T(8,128)(2,1)S(1)}, bf16[2,384,256]{2,1,0:T(8,128)(2,1)S(1)}, bf16[2,512,256]{2,1,...) custom-call(bf16[2,1024,256]{2,1,0:T(8,128)(2,1)} %get-tuple-element, ...), custom_call_target="tpu_custom_call" | custom-call | tf_op jit(solution)/shard_map/prepare/pallas_call | solution.py:211
  39.8 1.4 %pad_add_fusion.3 = s32[2]{0:T(128)S(1)} fusion(s32[1]{0:T(128)} %bitcast.20, s32[1]{0:T(128)} %bitcast.18), kind=kLoop, calls=%fused_computation.84 | loop fusion | flops 2 | bytes 16 | tf_op jit(solution)/shard_map/stack | solution.py:422
  41.2 1.5 %collective-permute-start.37 = (s32[2]{0:T(128)S(1)}, s32[2]{0:T(128)S(1)}, u32[]{:S(2)}, u32[]{:S(2)}) collective-permute-start(s32[2]{0:T(128)S(1)} %pad_add_fusion.3), channel_id=1, source_target_pairs={{0,16},{16,0},{1,17},{17,1},{2,18},{18,2},{3,19},{19,3},{4,20},{20... | collective-permute-start | bytes 32 | tf_op jit(solution)/shard_map/ppermute | solution.py:431
  42.8 2.0 %collective-permute-done.37 = s32[2]{0:T(128)S(1)} collective-permute-done((s32[2]{0:T(128)S(1)}, s32[2]{0:T(128)S(1)}, u32[]{:S(2)}, u32[]{:S(2)}) %collective-permute-start.37) | collective-permute-done | bytes 40 | tf_op jit(solution)/shard_map/ppermute | solution.py:431
  44.7 1.3 %fusion.61 = s32[2]{0:T(128)S(1)} fusion(s32[2]{0:T(128)S(1)} %collective-permute-done.37, s32[1]{0:T(128)} %bitcast.20, s32[1]{0:T(128)} %bitcast.18), kind=kLoop, calls=%fused_computation.97 | loop fusion | flops 4 | bytes 24 | tf_op jit(solution)/shard_map/max | solution.py:429
  49.4 2.7 %place.1 = bf16[24,2,2048]{2,1,0:T(2,128)(2,1)} custom-call(s32[76]{0:T(128)S(1)} %pad_add_fusion.4.plan, bf16[16,2,2048]{2,1,0:T(2,128)(2,1)} %copy-done.7, bf16[16,2,2048]{2,1,0:T(2,128)(2,1)} %copy-done.33, bf16[16,2,2048]{2,1,0:T(2,128)(2,1)} %copy-done.34, bf16[16,2,2048]{2,1,0:T(2,128)(2,1)} %copy-done.35), custom_call_target="tpu_custom_call" | custom-call | tf_op jit(solution)/shard_map/place/pallas_call | solution.py:333
  52.1 13.2 %collective-permute-done.38.refs_0_ = bf16[2,1152,256]{2,1,0:T(8,128)(2,1)} collective-permute-done((bf16[2,1152,256]{2,1,0:T(8,128)(2,1)}, bf16[2,1152,256]{2,1,0:T(8,128)(2,1)}, u32[]{:S(2)}, u32[]{:S(2)}) %collective-permute-start.38) | collective-permute-done | bytes 1179680 | tf_op jit(solution)/shard_map/ppermute | solution.py:380
  65.3 2.2 %collective-permute-start.42 = (bf16[2,1152,256]{2,1,0:T(8,128)(2,1)}, bf16[2,1152,256]{2,1,0:T(8,128)(2,1)S(1)}, u32[]{:S(2)}, u32[]{:S(2)}) collective-permute-start(bf16[2,1152,256]{2,1,0:T(8,128)(2,1)} %collective-permute-done.38.refs_0_), channel_id=1, source_target_pairs={{0,8},{1,9},{4,12},{5,13},{8,0},{9,1},{12,4},{13,5},{16,24},{17,25... | collective-permute-start | bytes 3538952 | tf_op jit(solution)/shard_map/ppermute | solution.py:388
  67.5 1.3 %collective-permute-start.43 = (bf16[24,2,2048]{2,1,0:T(2,128)(2,1)}, bf16[24,2,2048]{2,1,0:T(2,128)(2,1)}, u32[]{:S(2)}, u32[]{:S(2)}) collective-permute-start(bf16[24,2,2048]{2,1,0:T(2,128)(2,1)} %place.1), channel_id=1, source_target_pairs={{2,0},{3,1},{6,4},{7,5},{10,8},{11,9},{14,12},{15,13},{18,16},{19,... | collective-permute-start | bytes 589832 | tf_op jit(solution)/shard_map/ppermute | solution.py:380
  70.8 29.6 %conditional.1 = (bf16[24,2,256,256]{3,2,1,0:T(8,128)(2,1)}, bf16[2,1152,256]{2,1,0:T(8,128)(2,1)}) conditional(s32[]{:T(128)} %clamp.3, (bf16[2,1152,256]{2,1,0:T(8,128)(2,1)}, bf16[24,2,256,256]{3,2,1,0:T(8,128)(2,1)}) %tuple.60, (bf16[2,128,256]{2,1,0:T(8,128)(2,1)S(1)}, s32[76]{0:T(128)S(1)}, ...), branch_computations={%region_13.14_spmd, %region_14.15_spmd, %region_15.16_spmd, %regio... | conditional | bytes 38273352 | solution.py:483
  70.9 2.1 %collective-permute-start.9 = (bf16[2,1152,256]{2,1,0:T(8,128)(2,1)}, bf16[2,1152,256]{2,1,0:T(8,128)(2,1)}, u32[]{:S(2)}, u32[]{:S(2)}) collective-permute-start(bf16[2,1152,256]{2,1,0:T(8,128)(2,1)} %get-tuple-element.97), channel_id=1, source_target_pairs={{0,4},{1,5},{4,0},{5,1},{8,12},{9,13},{12,8},{13,9},{16,20},{17,21... | collective-permute-start | bytes 3538952 | tf_op jit(solution)/shard_map/cond/branch_3_fun/ppermute | solution.py:388
  72.9 1.3 %collective-permute-start.7 = (bf16[2,384,256]{2,1,0:T(8,128)(2,1)S(1)}, bf16[2,384,256]{2,1,0:T(8,128)(2,1)S(1)}, u32[]{:S(2)}, u32[]{:S(2)}) collective-permute-start(bf16[2,384,256]{2,1,0:T(8,128)(2,1)S(1)} %get-tuple-element.95), channel_id=1, source_target_pairs={{2,0},{3,1},{6,4},{7,5},{10,8},{11,9},{14,12},{15,13},{18,16},{19,... | collective-permute-start | bytes 1179656 | tf_op jit(solution)/shard_map/cond/branch_3_fun/ppermute | solution.py:380
  74.2 19.4 %collective-permute-done.7.refs_0_ = bf16[2,384,256]{2,1,0:T(8,128)(2,1)S(1)} collective-permute-done((bf16[2,384,256]{2,1,0:T(8,128)(2,1)S(1)}, bf16[2,384,256]{2,1,0:T(8,128)(2,1)S(1)}, u32[]{:S(2)}, u32[]{:S(2)}) %collective-permute-start.7) | collective-permute-done | bytes 393248 | tf_op jit(solution)/shard_map/cond/branch_3_fun/ppermute | solution.py:380
  93.6 1.9 %collective-permute-start.8 = (bf16[2,384,256]{2,1,0:T(8,128)(2,1)S(1)}, bf16[2,384,256]{2,1,0:T(8,128)(2,1)S(1)}, u32[]{:S(2)}, u32[]{:S(2)}) collective-permute-start(bf16[2,384,256]{2,1,0:T(8,128)(2,1)S(1)} %collective-permute-done.7.refs_0_), channel_id=1, source_target_pairs={{0,4},{1,5},{4,0},{5,1},{8,12},{9,13},{12,8},{13,9},{16,20},{17,21... | collective-permute-start | bytes 1179656 | tf_op jit(solution)/shard_map/cond/branch_3_fun/ppermute | solution.py:388
  95.6 1.7 %collective-permute-done.8.refs_1_ = bf16[2,384,256]{2,1,0:T(8,128)(2,1)S(1)} collective-permute-done((bf16[2,384,256]{2,1,0:T(8,128)(2,1)S(1)}, bf16[2,384,256]{2,1,0:T(8,128)(2,1)S(1)}, u32[]{:S(2)}, u32[]{:S(2)}) %collective-permute-start.8) | collective-permute-done | bytes 393248 | tf_op jit(solution)/shard_map/cond/branch_3_fun/ppermute | solution.py:388
  98.0 2.4 %unpack.13 = bf16[24,2,256,256]{3,2,1,0:T(8,128)(2,1)} custom-call(s32[76]{0:T(128)S(1)} %get-tuple-element.94.plan, bf16[2,384,256]{2,1,0:T(8,128)(2,1)} %copy-done.27, bf16[2,384,256]{2,1,0:T(8,128)(2,1)} %copy-done.28, bf16[24,2,256,256]{3,2,1,0:T(8,128)(2,1)} %get-tuple-element.96.refs_2_), custom_call_target="tpu_custom_call", output_to_operand_aliasing={{}: (3, {})} | custom-call | tf_op jit(solution)/shard_map/cond/branch_3_fun/unpack/pallas_call | solution.py:293
  100.4 2.0 %collective-permute-start.44 = (bf16[2,1152,256]{2,1,0:T(8,128)(2,1)S(1)}, bf16[2,1152,256]{2,1,0:T(8,128)(2,1)S(1)}, u32[]{:S(2)}, u32[]{:S(2)}) collective-permute-start(bf16[2,1152,256]{2,1,0:T(8,128)(2,1)S(1)} %collective-permute-done.42.refs_2_), channel_id=1, source_target_pairs={{0,4},{1,5},{4,0},{5,1},{8,12},{9,13},{12,8},{13,9},{16,20},{17,21... | collective-permute-start | bytes 3538952 | tf_op jit(solution)/shard_map/ppermute | solution.py:388
  103.2 2.0 %collective-permute-done.44.refs_3_ = bf16[2,1152,256]{2,1,0:T(8,128)(2,1)S(1)} collective-permute-done((bf16[2,1152,256]{2,1,0:T(8,128)(2,1)S(1)}, bf16[2,1152,256]{2,1,0:T(8,128)(2,1)S(1)}, u32[]{:S(2)}, u32[]{:S(2)}) %collective-permute-start.44) | collective-permute-done | bytes 1179680 | tf_op jit(solution)/shard_map/ppermute | solution.py:388
  105.2 1.0 copy-done.6
  106.2 3.1 %unpack.21 = bf16[24,2,256,256]{3,2,1,0:T(8,128)(2,1)} custom-call(s32[76]{0:T(128)S(1)} %pad_add_fusion.4.plan, bf16[2,1152,256]{2,1,0:T(8,128)(2,1)} %collective-permute-done.38.refs_0_, bf16[2,1152,256]{2,1,0:T(8,128)(2,1)} %get-tuple-element.196.refs_1_, bf16[2,1152,256]{2,1,0:T(8,128)(2,1)} %copy-done.5, ...), custom_call_target="tpu_custom_call", output_to_operand_aliasing={{}: (5, {})} | custom-call | tf_op jit(solution)/shard_map/unpack/pallas_call | solution.py:293
  109.3 1.7 %copy.153 = bf16[1,1,24,2,2048]{4,3,2,1,0:T(2,128)(2,1)} copy(bf16[1,1,24,2,2048]{4,3,2,1,0:T(2,128)(2,1)} %bitcast.27) | data formatting | bytes 393216
  (96 shorter events, 11.1 us)
Async XLA Ops:
  0.6 5.9 %copy-start.38 = (s32[16]{0:T(128)S(1)}, s32[16]{0:T(128)}, u32[]{:S(2)}) copy-start(s32[16]{0:T(128)} %lens.1) | copy-start | bytes 196
  0.6 10.6 %copy-start = (bf16[48,64,256]{2,1,0:T(8,128)(2,1)S(1)}, bf16[48,64,256]{2,1,0:T(8,128)(2,1)}, u32[]{:S(2)}) copy-start(bf16[48,64,256]{2,1,0:T(8,128)(2,1)} %keys.1) | copy-start | bytes 4718596
  0.7 10.3 %copy-start.37 = (s32[16,4]{0,1:T(4,128)S(1)}, s32[16,4]{0,1:T(4,128)}, u32[]{:S(2)}) copy-start(s32[16,4]{0,1:T(4,128)} %param.25) | copy-start | bytes 772
  0.7 5.9 %copy-start.39 = (s32[16,1]{0,1:T(1,128)S(1)}, s32[16,1]{0,1:T(1,128)}, u32[]{:S(2)}) copy-start(s32[16,1]{0,1:T(1,128)} %param.27) | copy-start | bytes 196
  6.5 26.0 %collective-permute-start.35 = (s32[1,2,16]{2,0,1:T(1,128)S(1)}, s32[1,2,16]{2,0,1:T(1,128)S(1)}, u32[]{:S(2)}, u32[]{:S(2)}) collective-permute-start(s32[1,2,16]{2,0,1:T(1,128)S(1)} %bitcast.77), channel_id=1, source_target_pairs={{0,8},{4,12},{8,0},{12,4},{1,9},{5,13},{9,1},{13,5},{2,10},{6,14},... | collective-permute-start | bytes 392 | tf_op jit(solution)/shard_map/ppermute | solution.py:417
  9.6 55.7 %collective-permute-start.38 = (bf16[2,1152,256]{2,1,0:T(8,128)(2,1)}, bf16[2,1152,256]{2,1,0:T(8,128)(2,1)}, u32[]{:S(2)}, u32[]{:S(2)}) collective-permute-start(bf16[2,1152,256]{2,1,0:T(8,128)(2,1)} %get-tuple-element.180), channel_id=1, source_target_pairs={{2,0},{3,1},{6,4},{7,5},{10,8},{11,9},{14,12},{15,13},{18,16},{19,... | collective-permute-start | bytes 3538952 | tf_op jit(solution)/shard_map/ppermute | solution.py:380
  11.2 2.0 %copy-start.1 = (bf16[48,64,256]{2,1,0:T(8,128)(2,1)S(1)}, bf16[48,64,256]{2,1,0:T(8,128)(2,1)}, u32[]{:S(2)}) copy-start(bf16[48,64,256]{2,1,0:T(8,128)(2,1)} %values.1) | copy-start | bytes 4718596
  13.2 2.0 %copy-start.36 = (bf16[16,2,2048]{2,1,0:T(2,128)(2,1)S(1)}, bf16[16,2,2048]{2,1,0:T(2,128)(2,1)}, u32[]{:S(2)}) copy-start(bf16[16,2,2048]{2,1,0:T(2,128)(2,1)} %param.22) | copy-start | bytes 393220
  13.2 2.2 %copy-start.4 = (bf16[16,2,8192]{2,1,0:T(2,128)(2,1)S(1)}, bf16[16,2,8192]{2,1,0:T(2,128)(2,1)}, u32[]{:S(2)}) copy-start(bf16[16,2,8192]{2,1,0:T(2,128)(2,1)} %param.21) | copy-start | bytes 1572868
  18.7 3.3 %copy-start.3 = (bf16[64,64,256]{2,1,0:T(8,128)(2,1)S(1)}, bf16[64,64,256]{2,1,0:T(8,128)(2,1)}, u32[]{:S(2)}) copy-start(bf16[64,64,256]{2,1,0:T(8,128)(2,1)} %gather_fusion.1) | copy-start | bytes 6291460
  24.4 3.8 %copy-start.2 = (bf16[64,64,256]{2,1,0:T(8,128)(2,1)S(1)}, bf16[64,64,256]{2,1,0:T(8,128)(2,1)}, u32[]{:S(2)}) copy-start(bf16[64,64,256]{2,1,0:T(8,128)(2,1)} %gather_fusion) | copy-start | bytes 6291460
  28.1 2.0 %copy-start.40 = (s32[4]{0:T(128)S(1)}, s32[4]{0:T(128)}, u32[]{:S(2)}) copy-start(s32[4]{0:T(128)} %constant.105.clone) | copy-start | bytes 52
  32.6 4.5 %collective-permute-start.36 = (s32[2,2,16]{2,0,1:T(2,128)S(1)}, s32[2,2,16]{2,0,1:T(2,128)S(1)}, u32[]{:S(2)}, u32[]{:S(2)}) collective-permute-start(s32[2,2,16]{2,0,1:T(2,128)S(1)} %pad_add_fusion.1), channel_id=1, source_target_pairs={{0,4},{4,0},{8,12},{12,8},{1,5},{5,1},{9,13},{13,9},{2,6},{6,2},{1... | collective-permute-start | bytes 776 | tf_op jit(solution)/shard_map/ppermute | solution.py:417
  32.7 15.5 %copy-start.7 = (bf16[16,2,2048]{2,1,0:T(2,128)(2,1)}, bf16[16,2,2048]{2,1,0:T(2,128)(2,1)S(1)}, u32[]{:S(2)}) copy-start(bf16[16,2,2048]{2,1,0:T(2,128)(2,1)S(1)} %convert_element_type.52.refs_0_) | copy-start | bytes 393220
  41.2 3.5 %collective-permute-start.37 = (s32[2]{0:T(128)S(1)}, s32[2]{0:T(128)S(1)}, u32[]{:S(2)}, u32[]{:S(2)}) collective-permute-start(s32[2]{0:T(128)S(1)} %pad_add_fusion.3), channel_id=1, source_target_pairs={{0,16},{16,0},{1,17},{17,1},{2,18},{18,2},{3,19},{19,3},{4,20},{20... | collective-permute-start | bytes 32 | tf_op jit(solution)/shard_map/ppermute | solution.py:431
  46.1 1.3 %collective-permute-start.39 = (bf16[16,2,2048]{2,1,0:T(2,128)(2,1)S(1)}, bf16[16,2,2048]{2,1,0:T(2,128)(2,1)S(1)}, u32[]{:S(2)}, u32[]{:S(2)}) collective-permute-start(bf16[16,2,2048]{2,1,0:T(2,128)(2,1)S(1)} %convert_element_type.52.refs_0_), channel_id=1, source_target_pairs={{2,10},{3,11},{6,14},{7,15},{10,2},{11,3},{14,6},{15,7},{18,26},{1... | collective-permute-start | bytes 393224 | tf_op jit(solution)/shard_map/ppermute | solution.py:388
  46.7 1.4 %collective-permute-start.40 = (bf16[16,2,2048]{2,1,0:T(2,128)(2,1)S(1)}, bf16[16,2,2048]{2,1,0:T(2,128)(2,1)S(1)}, u32[]{:S(2)}, u32[]{:S(2)}) collective-permute-start(bf16[16,2,2048]{2,1,0:T(2,128)(2,1)S(1)} %convert_element_type.52.refs_0_), channel_id=1, source_target_pairs={{2,6},{3,7},{6,2},{7,3},{10,14},{11,15},{14,10},{15,11},{18,22},{1... | collective-permute-start | bytes 393224 | tf_op jit(solution)/shard_map/ppermute | solution.py:388
  47.4 0.7 copy-start.33
  47.4 0.7 collective-permute-start.41
  48.1 0.6 copy-start.34
  48.8 0.7 copy-start.35
  65.3 35.1 %collective-permute-start.42 = (bf16[2,1152,256]{2,1,0:T(8,128)(2,1)}, bf16[2,1152,256]{2,1,0:T(8,128)(2,1)S(1)}, u32[]{:S(2)}, u32[]{:S(2)}) collective-permute-start(bf16[2,1152,256]{2,1,0:T(8,128)(2,1)} %collective-permute-done.38.refs_0_), channel_id=1, source_target_pairs={{0,8},{1,9},{4,12},{5,13},{8,0},{9,1},{12,4},{13,5},{16,24},{17,25... | collective-permute-start | bytes 3538952 | tf_op jit(solution)/shard_map/ppermute | solution.py:388
  67.5 32.9 %collective-permute-start.43 = (bf16[24,2,2048]{2,1,0:T(2,128)(2,1)}, bf16[24,2,2048]{2,1,0:T(2,128)(2,1)}, u32[]{:S(2)}, u32[]{:S(2)}) collective-permute-start(bf16[24,2,2048]{2,1,0:T(2,128)(2,1)} %place.1), channel_id=1, source_target_pairs={{2,0},{3,1},{6,4},{7,5},{10,8},{11,9},{14,12},{15,13},{18,16},{19,... | collective-permute-start | bytes 589832 | tf_op jit(solution)/shard_map/ppermute | solution.py:380
  70.8 31.6 %copy-start.8 = (bf16[16,2,2048]{2,1,0:T(2,128)(2,1)S(1)}, bf16[16,2,2048]{2,1,0:T(2,128)(2,1)}, u32[]{:S(2)}) copy-start(bf16[16,2,2048]{2,1,0:T(2,128)(2,1)} %copy-done.7) | copy-start | bytes 393220
  70.9 29.5 %collective-permute-start.9 = (bf16[2,1152,256]{2,1,0:T(8,128)(2,1)}, bf16[2,1152,256]{2,1,0:T(8,128)(2,1)}, u32[]{:S(2)}, u32[]{:S(2)}) collective-permute-start(bf16[2,1152,256]{2,1,0:T(8,128)(2,1)} %get-tuple-element.97), channel_id=1, source_target_pairs={{0,4},{1,5},{4,0},{5,1},{8,12},{9,13},{12,8},{13,9},{16,20},{17,21... | collective-permute-start | bytes 3538952 | tf_op jit(solution)/shard_map/cond/branch_3_fun/ppermute | solution.py:388
  72.9 20.7 %collective-permute-start.7 = (bf16[2,384,256]{2,1,0:T(8,128)(2,1)S(1)}, bf16[2,384,256]{2,1,0:T(8,128)(2,1)S(1)}, u32[]{:S(2)}, u32[]{:S(2)}) collective-permute-start(bf16[2,384,256]{2,1,0:T(8,128)(2,1)S(1)} %get-tuple-element.95), channel_id=1, source_target_pairs={{2,0},{3,1},{6,4},{7,5},{10,8},{11,9},{14,12},{15,13},{18,16},{19,... | collective-permute-start | bytes 1179656 | tf_op jit(solution)/shard_map/cond/branch_3_fun/ppermute | solution.py:380
  93.6 3.6 %copy-start.27 = (bf16[2,384,256]{2,1,0:T(8,128)(2,1)}, bf16[2,384,256]{2,1,0:T(8,128)(2,1)S(1)}, u32[]{:S(2)}) copy-start(bf16[2,384,256]{2,1,0:T(8,128)(2,1)S(1)} %collective-permute-done.7.refs_0_) | copy-start | bytes 1179652 | tf_op jit(solution)/shard_map/cond
  93.6 3.6 %collective-permute-start.8 = (bf16[2,384,256]{2,1,0:T(8,128)(2,1)S(1)}, bf16[2,384,256]{2,1,0:T(8,128)(2,1)S(1)}, u32[]{:S(2)}, u32[]{:S(2)}) collective-permute-start(bf16[2,384,256]{2,1,0:T(8,128)(2,1)S(1)} %collective-permute-done.7.refs_0_), channel_id=1, source_target_pairs={{0,4},{1,5},{4,0},{5,1},{8,12},{9,13},{12,8},{13,9},{16,20},{17,21... | collective-permute-start | bytes 1179656 | tf_op jit(solution)/shard_map/cond/branch_3_fun/ppermute | solution.py:388
  97.2 0.7 copy-start.28
  100.4 4.8 %copy-start.5 = (bf16[2,1152,256]{2,1,0:T(8,128)(2,1)}, bf16[2,1152,256]{2,1,0:T(8,128)(2,1)S(1)}, u32[]{:S(2)}) copy-start(bf16[2,1152,256]{2,1,0:T(8,128)(2,1)S(1)} %collective-permute-done.42.refs_2_) | copy-start | bytes 3538948
  100.4 4.7 %collective-permute-start.44 = (bf16[2,1152,256]{2,1,0:T(8,128)(2,1)S(1)}, bf16[2,1152,256]{2,1,0:T(8,128)(2,1)S(1)}, u32[]{:S(2)}, u32[]{:S(2)}) collective-permute-start(bf16[2,1152,256]{2,1,0:T(8,128)(2,1)S(1)} %collective-permute-done.42.refs_2_), channel_id=1, source_target_pairs={{0,4},{1,5},{4,0},{5,1},{8,12},{9,13},{12,8},{13,9},{16,20},{17,21... | collective-permute-start | bytes 3538952 | tf_op jit(solution)/shard_map/ppermute | solution.py:388
  105.2 1.0 copy-start.6

commit v2 on v1

--- a/solution.py
+++ b/solution.py
@@ -14,6 +14,7 @@
 ANY = pl.BlockSpec(memory_space=pl.ANY)
 HBM = pl.BlockSpec(memory_space=pltpu.HBM)
 VMEM_LIMIT = 60 * 1024 * 1024
+UNPACK_LIMIT = 12 * 1024 * 1024
 
 
 def rotate(values, positions):
@@ -191,8 +192,8 @@
     load.start()
     blank[...] = jnp.zeros_like(blank)
     copies = [
-        pltpu.make_async_copy(blank, pool.at[slot], pool_sems.at[slot])
-        for slot in range(pool.shape[0])
+        pltpu.make_async_copy(blank, pool.at[0, 0, slot], pool_sems.at[slot])
+        for slot in range(pool.shape[2])
     ]
     for copy in copies:
         copy.start()
@@ -201,7 +202,7 @@
         pltpu.make_async_copy(held.at[:, pl.ds(0, part.shape[1]), :], part, sems.at[number])
         for number, part in enumerate(parts)
     ]
-    for copy in copies[pool.shape[0] :]:
+    for copy in copies[pool.shape[2] :]:
         copy.start()
     for copy in copies:
         copy.wait()
@@ -218,10 +219,10 @@
         out_specs=[HBM] * (len(sizes) + 1),
         scratch_shapes=[
             pltpu.VMEM(pile.shape, pile.dtype),
-            pltpu.VMEM(pool_shape[1:], pile.dtype),
+            pltpu.VMEM(pool_shape[3:], pile.dtype),
             pltpu.SemaphoreType.DMA,
             pltpu.SemaphoreType.DMA((len(sizes),)),
-            pltpu.SemaphoreType.DMA((pool_shape[0],)),
+            pltpu.SemaphoreType.DMA((pool_shape[2],)),
         ],
         compiler_params=pltpu.CompilerParams(vmem_limit_bytes=VMEM_LIMIT),
         name="prepare",
@@ -233,31 +234,34 @@
     return plan[count + (kind * count + j) * capacity + c]
 
 
-def unpack_kernel(low, high, total, capacity, numbers, plan, *refs):
+def unpack_kernel(extents, total, capacity, numbers, plan, *refs):
     count = len(numbers)
     piles, out, stage, inward, outward = refs[:count], refs[-4], refs[-3], refs[-2], refs[-1]
 
-    def span(j, c):
+    def span(k, c):
+        j, (low, high) = numbers[k], extents[k]
         start = entry(plan, total, capacity, 0, j, c)
         begin = jnp.maximum(start, low)
         end = jnp.minimum(start + entry(plan, total, capacity, 1, j, c), high)
         return start, begin, end - begin
 
     def arriving(k, c):
-        _, begin, rows = span(numbers[k], c)
+        _, begin, rows = span(k, c)
         rows = pl.multiple_of(rows, UNIT)
         return pltpu.make_async_copy(
-            piles[k].at[:, pl.ds(pl.multiple_of(begin - low, UNIT), rows), :],
+            piles[k].at[:, pl.ds(pl.multiple_of(begin - extents[k][0], UNIT), rows), :],
             stage.at[k * capacity + c, :, pl.ds(0, rows), :],
             inward.at[k * capacity + c],
         )
 
     def leaving(k, c):
-        start, begin, rows = span(numbers[k], c)
+        start, begin, rows = span(k, c)
         rows = pl.multiple_of(rows, UNIT)
         return pltpu.make_async_copy(
             stage.at[k * capacity + c, :, pl.ds(0, rows), :],
             out.at[
+                0,
+                0,
                 plan[numbers[k]] * capacity + c,
                 :,
                 pl.ds(pl.multiple_of(begin - start, UNIT), rows),
@@ -270,7 +274,7 @@
         for k in range(count):
 
             def slot(c, carry):
-                @pl.when(span(numbers[k], c)[2] > 0)
+                @pl.when(span(k, c)[2] > 0)
                 def _():
                     action(k, c)
 
@@ -287,11 +291,12 @@
     each(lambda k, c: leaving(k, c).wait())
 
 
-def unpack(plan, total, capacity, parts, out, low, high):
+def unpack(plan, total, capacity, parts, out):
     count = len(parts)
-    numbers = [number for _, number in parts]
+    numbers = [part[1] for part in parts]
+    extents = [part[2:] for part in parts]
     return pl.pallas_call(
-        functools.partial(unpack_kernel, low, high, total, capacity, numbers),
+        functools.partial(unpack_kernel, extents, total, capacity, numbers),
         out_shape=jax.ShapeDtypeStruct(out.shape, out.dtype),
         grid_spec=pltpu.PrefetchScalarGridSpec(
             num_scalar_prefetch=1,
@@ -299,15 +304,15 @@
             in_specs=[ANY] * count + [HBM],
             out_specs=HBM,
             scratch_shapes=[
-                pltpu.VMEM((count * capacity,) + out.shape[1:], out.dtype),
+                pltpu.VMEM((count * capacity,) + out.shape[3:], out.dtype),
                 pltpu.SemaphoreType.DMA((count * capacity,)),
                 pltpu.SemaphoreType.DMA((count * capacity,)),
             ],
         ),
         input_output_aliases={1 + count: 0},
-        compiler_params=pltpu.CompilerParams(vmem_limit_bytes=VMEM_LIMIT),
+        compiler_params=pltpu.CompilerParams(vmem_limit_bytes=UNPACK_LIMIT),
         name="unpack",
-    )(plan, *[pile for pile, _ in parts], out)
+    )(plan, *[part[0] for part in parts], out)
 
 
 def place_kernel(total, capacity, numbers, plan, *refs):
@@ -454,45 +459,44 @@
     plan_shape = (instances, capacity)
 
     local_output = attend(own_keys, own_values, cache_length, queries, own_fresh_k, own_fresh_v)
-    near_sizes = list(range(step, most - cut, step)) + [most - cut]
-    far_sizes = list(range(4 * step, most - cut, 4 * step)) + [most - cut]
-    rests, pool = prepare(rest, near_sizes, (slot_count, 2, span_rows, group_width))
+    near_sizes = list(range(2 * step, (most - cut) * 3 // 4, step)) + [most - cut]
+    far_sizes = near_sizes[2::2]
+    rests, pool = prepare(rest, near_sizes, (1, 1, slot_count, 2, span_rows, group_width))
     local_output, pool, rests, extents, plan = lax.optimization_barrier(
         (local_output, pool, rests, extents, plan)
     )
-    inherited = place(plan, *plan_shape, spread(local_output, all_steps, halved_count))
-    first, inherited = lax.optimization_barrier((first, inherited))
-    inherited = down(inherited)
-    far_first = across(first, all_steps[0], 0)
-
-    def finish(more, far, rests, first, plan, pool):
-        if more:
-            piece = down(rests[near_sizes.index(more)])
-        near_first = [part for part, _ in spread(first, all_steps[1:])[1:]]
-        if more:
-            pieces = spread(piece, all_steps if far else all_steps[1:])
-            pool = unpack(plan, *plan_shape, pieces, pool, cut, cut + more)
-        return pool, near_first
-
-    branches = [functools.partial(finish, more, False) for more in [0] + near_sizes]
+    local_rows = local_output
+    local_output = jnp.where(remaining_device, local_output, jnp.zeros_like(local_output))
+    first, local_rows, local_output = lax.optimization_barrier((first, local_rows, local_output))
+
+    def finish(more, far, rests, first, local_rows, plan, pool):
+        piece = down(rests[near_sizes.index(more)])
+        away = across(first, all_steps[0], 0)
+        inherited = place(plan, *plan_shape, spread(local_rows, all_steps, halved_count))
+        inherited = down(inherited)
+        inherited = jnp.where(remaining_device, inherited, jnp.zeros_like(inherited))
+        parts = [part + (0, cut) for part in spread(first, all_steps[1:])]
+        pool = unpack(plan, *plan_shape, parts, pool)
+        away, piece, pool, inherited = lax.optimization_barrier((away, piece, pool, inherited))
+        parts = [
+            (part, order.index(order[number] ^ all_steps[0]), 0, cut)
+            for part, number in spread(away, all_steps[1:])
+        ]
+        pieces = [
+            part + (cut, cut + more)
+            for part in spread(piece, all_steps if far else all_steps[1:])
+        ]
+        pool = unpack(plan, *plan_shape, [parts[0], pieces[0]], pool)
+        return inherited, unpack(plan, *plan_shape, parts[1:] + pieces[1:], pool)
+
+    branches = [functools.partial(finish, more, False) for more in near_sizes]
     branches += [functools.partial(finish, more, True) for more in far_sizes]
     extra = jnp.maximum(extents[0] - cut, 0)
-    near_choice = jnp.minimum((extra + step - 1) // step, len(near_sizes))
-    far_choice = jnp.clip((extra + 4 * step - 1) // (4 * step) - 1, 0, len(far_sizes) - 1)
-    choice = jnp.where(extents[1] > cut, 1 + len(near_sizes) + far_choice, near_choice)
-    pool, near_first = lax.switch(choice, branches, rests, first, plan, pool)
-    far_first, pool, inherited = lax.optimization_barrier((far_first, pool, inherited))
-    places = [0]
-    for stride in all_steps[1:]:
-        places = places + [o ^ stride for o in places]
-    near_parts = [(part, order.index(o)) for part, o in zip([first] + near_first, places)]
-    far_parts = [
-        (part, order.index(order[number] ^ all_steps[0]))
-        for part, number in spread(far_first, all_steps[1:])
-    ]
-    kept_cache = unpack(plan, *plan_shape, near_parts + far_parts, pool, 0, cut)
-    local_output = jnp.where(remaining_device, local_output, jnp.zeros_like(local_output))
-    return (local_output, inherited[None, None], kept_cache[None, None])
+    near_choice = sum((extra > size).astype(jnp.int32) for size in near_sizes[:-1])
+    far_choice = sum((extra > size).astype(jnp.int32) for size in far_sizes[:-1])
+    choice = jnp.where(extents[1] > cut, len(near_sizes) + far_choice, near_choice)
+    inherited, kept_cache = lax.switch(choice, branches, rests, first, local_rows, plan, pool)
+    return (local_output, inherited[None, None], kept_cache)
 
 
 def solution(mesh):

time: 112 us -> 110 us (0.982)
  matrix products: 11.8 us -> 9.61 us
  local copies, waits for them, and re-layouts: 14.7 us -> 12.8 us
    dot_general x1, matrix products: 3.11 us -> 0.92 us  [new_tokens(): jnp.dot(flat_rows, weight_value, preferred_element_type=jnp.float32)]
    ppermute x3, waiting for transfers between devices: 32.6 us -> 34.5 us  [down(): lax.ppermute(value, 'tp', [(t + halved_count, t) for t in range(halved_co...]
    unnamed x35 -> x27, local copies, waits for them, and re-layouts: 4.06 us -> 2.16 us
    pallas_call x2 -> x3, Pallas kernels: 5.48 us -> 6.52 us  [unpack(): pl.pallas_call(functools.partial(unpack_kernel, extents, total, capacity,...]
  transfers between devices with their start and end apart: 13 -> 13, of which waited for: 5 -> 5; matrix products, arithmetic and copies ran while one was open for 26% -> 24% of each run, Pallas kernels for 8% -> 10%
where the time goes in v2:
time: 110 us; the launch traced here: 108 us
  waiting for transfers between devices  39.1 us (36%)
  starting transfers between devices  18.8 us (17%)
  Pallas kernels  18.7 us (17%)
  local copies, waits for them, and re-layouts  12.8 us (12%)
  matrix products  9.61 us (9%)
  other arithmetic  6.23 us (6%)
  between operations  2.35 us (2%)
    ppermute x3, waiting for transfers between devices, down(): lax.ppermute(value, 'tp', [(t + halved_count, t) for t in range(halved_co...  34.5 us
    ppermute x7, starting transfers between devices, across(): return lax.ppermute(value, ('inst', 'tp'), pairs)  10.4 us
    pallas_call x3, Pallas kernels, unpack(): pl.pallas_call(functools.partial(unpack_kernel, extents, total, capacity,...  6.52 us
    pallas_call x1, Pallas kernels, pack(): pl.pallas_call(functools.partial(pack_kernel, cuts, steps), out_shape=tup...  5.88 us
    ppermute x3, starting transfers between devices, down(): lax.ppermute(value, 'tp', [(t + halved_count, t) for t in range(halved_co...  3.85 us
    pallas_call x1, Pallas kernels, prepare(): pl.pallas_call(functools.partial(prepare_kernel, len(sizes)), out_shape=[...  3.6 us
    dot_general x1, matrix products, new_tokens(): jnp.dot(flat_rows, weight_key, preferred_element_type=jnp.float32)  3.16 us
    ppermute x2, starting transfers between devices, local(): lax.ppermute(facts, 'inst', [(i, i ^ stride) for i in range(instances)])  2.96 us
  transfers between devices with their start and end apart: 13, of which 5 were waited for; matrix products, arithmetic and copies ran while one was open for 24% of the time, Pallas kernels for 10%

profile of v2, /device:TPU:0, one launch (start us, length us, event | category | flops | bytes accessed | tf_op | source)
XLA Modules:
  0.0 108.0 jit_solution(16679929012913880971)
XLA Ops:
  0.7 5.9 %pack.1 = (bf16[2,1152,256]{2,1,0:T(8,128)(2,1)}, bf16[2,1024,256]{2,1,0:T(8,128)(2,1)}) custom-call(s32[4,16]{1,0:T(4,128)} %bitcast.79, s32[16]{0:T(128)} %lens.1, s32[16]{0:T(128)} %bitcast.81, bf16[48,64,256]{2,1,0:T(8,128)(2,1)} %keys.1, bf16[48,64,256]{2,1,0:T(8,128)(2,1)} %values.1), custom_call_target="tpu_custom_call" | custom-call | tf_op jit(solution)/shard_map/pack/pallas_call | solution.py:166
  6.6 2.9 %collective-permute-start.68 = (s32[1,2,16]{2,0,1:T(1,128)S(1)}, s32[1,2,16]{2,0,1:T(1,128)S(1)}, u32[]{:S(2)}, u32[]{:S(2)}) collective-permute-start(s32[1,2,16]{2,0,1:T(1,128)S(1)} %bitcast.76), channel_id=1, source_target_pairs={{0,8},{4,12},{8,0},{12,4},{1,9},{5,13},{9,1},{13,5},{2,10},{6,14},... | collective-permute-start | bytes 392 | tf_op jit(solution)/shard_map/ppermute | solution.py:422
  9.5 1.3 %collective-permute-start.67 = (bf16[2,1152,256]{2,1,0:T(8,128)(2,1)}, bf16[2,1152,256]{2,1,0:T(8,128)(2,1)}, u32[]{:S(2)}, u32[]{:S(2)}) collective-permute-start(bf16[2,1152,256]{2,1,0:T(8,128)(2,1)} %get-tuple-element.184), channel_id=1, source_target_pairs={{2,0},{3,1},{6,4},{7,5},{10,8},{11,9},{14,12},{15,13},{18,16},{19,... | collective-permute-start | bytes 3538952 | tf_op jit(solution)/shard_map/ppermute | solution.py:385
  11.1 2.0 %gather_fusion.1 = bf16[64,64,256]{2,1,0:T(8,128)(2,1)} fusion(bf16[48,64,256]{2,1,0:T(8,128)(2,1)S(1)} %copy-done, s32[1024]{0:T(1024)S(1)} %pad_clamp_fusion), kind=kCustom, calls=%fused_computation.1 | custom fusion | bytes 4194560 | tf_op jit(solution)/shard_map/gather | solution.py:415
  13.1 2.0 %gather_fusion = bf16[64,64,256]{2,1,0:T(8,128)(2,1)} fusion(bf16[48,64,256]{2,1,0:T(8,128)(2,1)S(1)} %copy-done.1, s32[1024]{0:T(1024)S(1)} %pad_clamp_fusion), kind=kCustom, calls=%fused_computation | custom fusion | bytes 4194560 | tf_op jit(solution)/shard_map/gather | solution.py:416
  15.3 3.2 %fusion.58 = f32[32,256]{1,0:T(8,128)S(1)} fusion(bf16[32,8192]{1,0:T(8,128)(2,1)S(1)} %reshape.184, bf16[8192,256]{1,0:T(8,128)(2,1)} %param.24), kind=kOutput, calls=%fused_computation.103 | convolution fusion | flops 134217728 | bytes 4751360 | tf_op jit(solution)/shard_map/dot_general | solution.py:42
  18.8 2.0 %reshape_reshape.7 = bf16[16,256,2,128]{3,2,1,0:T(2,128)(2,1)} reshape(bf16[64,64,256]{2,1,0:T(8,128)(2,1)S(1)} %copy-done.3) | data formatting | bytes 4194304 | tf_op jit(solution)/shard_map/reshape;reshape | solution.py:60
  21.2 2.5 %fusion.56 = (f32[16,2,2,8]{3,1,2,0:T(2,128)S(1)}, f32[16,2,2,8,256]{4,3,1,2,0:T(8,128)S(1)}) fusion(bf16[16,2,2,8,128]{4,3,2,1,0:T(8,128)(2,1)S(1)} %reshape.183, bf16[16,256,2,128,1]{3,2,1,0,4:T(2,128)(2,1)} %bitcast.73, pred[16,256]{1,0:T(8,128)(4,1)S(1)} %iota_compare_fusion), kind=kOutput, calls=%fused_computation.101 | convolution fusion | flops 33947136 | bytes 2758656 | tf_op jit(solution)/shard_map/sjgqe,stge->sjgqt/dot_general | solution.py:66
  25.0 0.9 fusion.26
  26.6 2.0 %reshape_reshape.6 = bf16[16,256,2,128]{3,2,1,0:T(2,128)(2,1)} reshape(bf16[64,64,256]{2,1,0:T(8,128)(2,1)S(1)} %copy-done.2) | data formatting | bytes 4194304 | tf_op jit(solution)/shard_map/reshape;reshape | solution.py:61
  28.9 2.0 %fusion.21 = bf16[16,2,2,8,128]{4,3,1,2,0:T(8,128)(2,1)S(1)} fusion(f32[16,2,128,2,8]{2,4,3,1,0:T(8,128)S(1)} %fusion.36, bf16[16,256,2,128,1]{3,2,1,0,4:T(2,128)(2,1)} %bitcast.72, f32[16,2,2,8,256]{4,3,1,2,0:T(8,128)S(1)} %get-tuple-element.367, f32[16,2,2,8]{3,1,2,0:T(2,128)S(1)} %add.85, f32[16,2,2,8]{3,1,2,0:T(2,128)S(1)} %max.14), kind=kOutput, calls=%fused_computation.20 | convolution fusion | flops 34078720 | bytes 3018752 | tf_op jit(solution)/shard_map/sjgqt,stge->sjgqe/dot_general | solution.py:83
  31.1 3.6 %prepare.1 = (bf16[2,256,256]{2,1,0:T(8,128)(2,1)S(1)}, bf16[2,384,256]{2,1,0:T(8,128)(2,1)}, bf16[2,512,256]{2,1,0:T(8,128)(2,1)S(1)}, bf16[2,640,256]{2,1,0:T(...) custom-call(bf16[2,1024,256]{2,1,0:T(8,128)(2,1)} %get-tuple-element.189.pile), custom_call_target="tpu_custom_call" | custom-call | tf_op jit(solution)/shard_map/prepare/pallas_call | solution.py:212
  37.5 1.4 %pad_add_fusion.3 = s32[2]{0:T(128)S(1)} fusion(s32[1]{0:T(128)} %bitcast.20, s32[1]{0:T(128)} %bitcast.18), kind=kLoop, calls=%fused_computation.91 | loop fusion | flops 2 | bytes 16 | tf_op jit(solution)/shard_map/stack | solution.py:427
  38.9 1.6 %collective-permute-start.70 = (s32[2]{0:T(128)S(1)}, s32[2]{0:T(128)S(1)}, u32[]{:S(2)}, u32[]{:S(2)}) collective-permute-start(s32[2]{0:T(128)S(1)} %pad_add_fusion.3), channel_id=1, source_target_pairs={{0,16},{16,0},{1,17},{17,1},{2,18},{18,2},{3,19},{19,3},{4,20},{20... | collective-permute-start | bytes 32 | tf_op jit(solution)/shard_map/ppermute | solution.py:436
  40.5 1.9 %collective-permute-done.70 = s32[2]{0:T(128)S(1)} collective-permute-done((s32[2]{0:T(128)S(1)}, s32[2]{0:T(128)S(1)}, u32[]{:S(2)}, u32[]{:S(2)}) %collective-permute-start.70) | collective-permute-done | bytes 40 | tf_op jit(solution)/shard_map/ppermute | solution.py:436
  42.4 1.4 %fusion.61 = s32[2]{0:T(128)S(1)} fusion(s32[2]{0:T(128)S(1)} %collective-permute-done.70, s32[1]{0:T(128)} %bitcast.20, s32[1]{0:T(128)} %bitcast.18), kind=kLoop, calls=%fused_computation.104 | loop fusion | flops 4 | bytes 24 | tf_op jit(solution)/shard_map/max | solution.py:434
  45.7 19.6 %collective-permute-done.67 = bf16[2,1152,256]{2,1,0:T(8,128)(2,1)} collective-permute-done((bf16[2,1152,256]{2,1,0:T(8,128)(2,1)}, bf16[2,1152,256]{2,1,0:T(8,128)(2,1)}, u32[]{:S(2)}, u32[]{:S(2)}) %collective-permute-start.67) | collective-permute-done | bytes 1179680 | tf_op jit(solution)/shard_map/ppermute | solution.py:385
  65.3 0.8 copy.105
  66.1 41.2 %conditional.1 = (bf16[24,2,2048]{2,1,0:T(2,128)(2,1)S(1)}, bf16[1,1,24,2,256,256]{5,4,3,2,1,0:T(8,128)(2,1)}) conditional(s32[]{:T(128)} %bitcast.24, (bf16[2,1152,256]{2,1,0:T(8,128)(2,1)}, bf16[2,256,256]{2,1,0:T(8,128)(2,1)S(1)}, s32[76]{0:T(128)S(1)}, bf16[1,1,24,2,256,256]{5,4,3,2,1,0:T(8,128)(2,1)}, ...), branch_computations={%region_13.14_spmd, %region_14.15_spmd, %region_15.16_spmd, %regio... | conditional | flops 98304 | bytes 36045368 | solution.py:498
  66.1 1.9 %collective-permute-start.11 = (bf16[2,1152,256]{2,1,0:T(8,128)(2,1)}, bf16[2,1152,256]{2,1,0:T(8,128)(2,1)S(1)}, u32[]{:S(2)}, u32[]{:S(2)}) collective-permute-start(bf16[2,1152,256]{2,1,0:T(8,128)(2,1)} %get-tuple-element.94.refs_0_), channel_id=1, source_target_pairs={{0,4},{1,5},{4,0},{5,1},{8,12},{9,13},{12,8},{13,9},{16,20},{17,21... | collective-permute-start | bytes 3538952 | tf_op jit(solution)/shard_map/cond/branch_1_fun/ppermute | solution.py:393
  68.0 2.2 %collective-permute-start.9 = (bf16[2,1152,256]{2,1,0:T(8,128)(2,1)}, bf16[2,1152,256]{2,1,0:T(8,128)(2,1)S(1)}, u32[]{:S(2)}, u32[]{:S(2)}) collective-permute-start(bf16[2,1152,256]{2,1,0:T(8,128)(2,1)} %get-tuple-element.94.refs_0_), channel_id=1, source_target_pairs={{0,8},{1,9},{4,12},{5,13},{8,0},{9,1},{12,4},{13,5},{16,24},{17,25... | collective-permute-start | bytes 3538952 | tf_op jit(solution)/shard_map/cond/branch_1_fun/ppermute | solution.py:393
  73.1 2.7 %place.8 = bf16[24,2,2048]{2,1,0:T(2,128)(2,1)} custom-call(s32[76]{0:T(128)S(1)} %get-tuple-element.96.plan, bf16[16,2,2048]{2,1,0:T(2,128)(2,1)} %copy-done.9, bf16[16,2,2048]{2,1,0:T(2,128)(2,1)} %copy-done.18, bf16[16,2,2048]{2,1,0:T(2,128)(2,1)} %copy-done.24, bf16[16,2,2048]{2,1,0:T(2,128)(2,1)} %copy-done.31), custom_call_target="tpu_custom_call" | custom-call | tf_op jit(solution)/shard_map/cond/branch_1_fun/place/pallas_call | solution.py:338
  75.8 1.3 %collective-permute-start.15 = (bf16[24,2,2048]{2,1,0:T(2,128)(2,1)}, bf16[24,2,2048]{2,1,0:T(2,128)(2,1)S(1)}, u32[]{:S(2)}, u32[]{:S(2)}) collective-permute-start(bf16[24,2,2048]{2,1,0:T(2,128)(2,1)} %place.8), channel_id=1, source_target_pairs={{2,0},{3,1},{6,4},{7,5},{10,8},{11,9},{14,12},{15,13},{18,16},{19,... | collective-permute-start | bytes 589832 | tf_op jit(solution)/shard_map/cond/branch_1_fun/ppermute | solution.py:385
  77.1 1.3 %collective-permute-start.10 = (bf16[2,384,256]{2,1,0:T(8,128)(2,1)}, bf16[2,384,256]{2,1,0:T(8,128)(2,1)S(1)}, u32[]{:S(2)}, u32[]{:S(2)}) collective-permute-start(bf16[2,384,256]{2,1,0:T(8,128)(2,1)} %get-tuple-element.95), channel_id=1, source_target_pairs={{2,0},{3,1},{6,4},{7,5},{10,8},{11,9},{14,12},{15,13},{18,16},{19,... | collective-permute-start | bytes 1179656 | tf_op jit(solution)/shard_map/cond/branch_1_fun/ppermute | solution.py:385
  78.4 9.4 %collective-permute-done.15 = bf16[24,2,2048]{2,1,0:T(2,128)(2,1)S(1)} collective-permute-done((bf16[24,2,2048]{2,1,0:T(2,128)(2,1)}, bf16[24,2,2048]{2,1,0:T(2,128)(2,1)S(1)}, u32[]{:S(2)}, u32[]{:S(2)}) %collective-permute-start.15) | collective-permute-done | bytes 196640 | tf_op jit(solution)/shard_map/cond/branch_1_fun/ppermute | solution.py:385
  88.0 2.3 %unpack.24.refs_2_ = bf16[1,1,24,2,256,256]{5,4,3,2,1,0:T(8,128)(2,1)} custom-call(s32[76]{0:T(128)S(1)} %get-tuple-element.96.plan, bf16[2,1152,256]{2,1,0:T(8,128)(2,1)} %get-tuple-element.94.refs_0_, bf16[2,1152,256]{2,1,0:T(8,128)(2,1)S(1)} %collective-permute-done.11.refs_1_, ...), custom_call_target="tpu_custom_call", output_to_operand_aliasing={{}: (3, {})} | custom-call | tf_op jit(solution)/shard_map/cond/branch_1_fun/unpack/pallas_call | solution.py:298
  90.3 5.5 %collective-permute-done.10.refs_1_ = bf16[2,384,256]{2,1,0:T(8,128)(2,1)S(1)} collective-permute-done((bf16[2,384,256]{2,1,0:T(8,128)(2,1)}, bf16[2,384,256]{2,1,0:T(8,128)(2,1)S(1)}, u32[]{:S(2)}, u32[]{:S(2)}) %collective-permute-start.10) | collective-permute-done | bytes 393248 | tf_op jit(solution)/shard_map/cond/branch_1_fun/ppermute | solution.py:385
  95.8 2.7 %collective-permute-done.9.refs_0_ = bf16[2,1152,256]{2,1,0:T(8,128)(2,1)S(1)} collective-permute-done((bf16[2,1152,256]{2,1,0:T(8,128)(2,1)}, bf16[2,1152,256]{2,1,0:T(8,128)(2,1)S(1)}, u32[]{:S(2)}, u32[]{:S(2)}) %collective-permute-start.9) | collective-permute-done | bytes 1179680 | tf_op jit(solution)/shard_map/cond/branch_1_fun/ppermute | solution.py:393
  98.5 1.9 %collective-permute-start.16 = (bf16[2,1152,256]{2,1,0:T(8,128)(2,1)S(1)}, bf16[2,1152,256]{2,1,0:T(8,128)(2,1)S(1)}, u32[]{:S(2)}, u32[]{:S(2)}) collective-permute-start(bf16[2,1152,256]{2,1,0:T(8,128)(2,1)S(1)} %collective-permute-done.9.refs_0_), channel_id=1, source_target_pairs={{0,4},{1,5},{4,0},{5,1},{8,12},{9,13},{12,8},{13,9},{16,20},{17,21... | collective-permute-start | bytes 3538952 | tf_op jit(solution)/shard_map/cond/branch_1_fun/ppermute | solution.py:393
  100.4 2.4 %collective-permute-start.17 = (bf16[2,384,256]{2,1,0:T(8,128)(2,1)S(1)}, bf16[2,384,256]{2,1,0:T(8,128)(2,1)S(1)}, u32[]{:S(2)}, u32[]{:S(2)}) collective-permute-start(bf16[2,384,256]{2,1,0:T(8,128)(2,1)S(1)} %collective-permute-done.10.refs_1_), channel_id=1, source_target_pairs={{0,4},{1,5},{4,0},{5,1},{8,12},{9,13},{12,8},{13,9},{16,20},{17,21... | collective-permute-start | bytes 1179656 | tf_op jit(solution)/shard_map/cond/branch_1_fun/ppermute | solution.py:393
  102.8 2.3 %unpack.25.refs_2_ = bf16[1,1,24,2,256,256]{5,4,3,2,1,0:T(8,128)(2,1)} custom-call(s32[76]{0:T(128)S(1)} %get-tuple-element.96.plan, bf16[2,1152,256]{2,1,0:T(8,128)(2,1)S(1)} %collective-permute-done.9.refs_0_, bf16[2,384,256]{2,1,0:T(8,128)(2,1)S(1)} %collective-permute-done.10.refs_1_, ...), custom_call_target="tpu_custom_call", output_to_operand_aliasing={{}: (3, {})} | custom-call | tf_op jit(solution)/shard_map/cond/branch_1_fun/unpack/pallas_call | solution.py:298
  105.1 2.0 %unpack.26 = bf16[1,1,24,2,256,256]{5,4,3,2,1,0:T(8,128)(2,1)} custom-call(s32[76]{0:T(128)S(1)} %get-tuple-element.96.plan, bf16[2,1152,256]{2,1,0:T(8,128)(2,1)S(1)} %collective-permute-done.16.refs_0_, bf16[2,384,256]{2,1,0:T(8,128)(2,1)S(1)} %collective-permute-done.17.refs_1_, ...), custom_call_target="tpu_custom_call", output_to_operand_aliasing={{}: (3, {})} | custom-call | tf_op jit(solution)/shard_map/cond/branch_1_fun/unpack/pallas_call | solution.py:298
  (95 shorter events, 10.6 us)
Async XLA Ops:
  0.6 10.3 %copy-start.37 = (s32[16,4]{0,1:T(4,128)S(1)}, s32[16,4]{0,1:T(4,128)}, u32[]{:S(2)}) copy-start(s32[16,4]{0,1:T(4,128)} %param.21) | copy-start | bytes 772
  0.6 5.9 %copy-start.39 = (s32[16,1]{0,1:T(1,128)S(1)}, s32[16,1]{0,1:T(1,128)}, u32[]{:S(2)}) copy-start(s32[16,1]{0,1:T(1,128)} %param.23) | copy-start | bytes 196
  0.7 10.5 %copy-start = (bf16[48,64,256]{2,1,0:T(8,128)(2,1)S(1)}, bf16[48,64,256]{2,1,0:T(8,128)(2,1)}, u32[]{:S(2)}) copy-start(bf16[48,64,256]{2,1,0:T(8,128)(2,1)} %keys.1) | copy-start | bytes 4718596
  0.7 5.9 %copy-start.38 = (s32[16]{0:T(128)S(1)}, s32[16]{0:T(128)}, u32[]{:S(2)}) copy-start(s32[16]{0:T(128)} %lens.1) | copy-start | bytes 196
  6.6 24.3 %collective-permute-start.68 = (s32[1,2,16]{2,0,1:T(1,128)S(1)}, s32[1,2,16]{2,0,1:T(1,128)S(1)}, u32[]{:S(2)}, u32[]{:S(2)}) collective-permute-start(s32[1,2,16]{2,0,1:T(1,128)S(1)} %bitcast.76), channel_id=1, source_target_pairs={{0,8},{4,12},{8,0},{12,4},{1,9},{5,13},{9,1},{13,5},{2,10},{6,14},... | collective-permute-start | bytes 392 | tf_op jit(solution)/shard_map/ppermute | solution.py:422
  9.5 55.8 %collective-permute-start.67 = (bf16[2,1152,256]{2,1,0:T(8,128)(2,1)}, bf16[2,1152,256]{2,1,0:T(8,128)(2,1)}, u32[]{:S(2)}, u32[]{:S(2)}) collective-permute-start(bf16[2,1152,256]{2,1,0:T(8,128)(2,1)} %get-tuple-element.184), channel_id=1, source_target_pairs={{2,0},{3,1},{6,4},{7,5},{10,8},{11,9},{14,12},{15,13},{18,16},{19,... | collective-permute-start | bytes 3538952 | tf_op jit(solution)/shard_map/ppermute | solution.py:385
  11.1 2.0 %copy-start.1 = (bf16[48,64,256]{2,1,0:T(8,128)(2,1)S(1)}, bf16[48,64,256]{2,1,0:T(8,128)(2,1)}, u32[]{:S(2)}) copy-start(bf16[48,64,256]{2,1,0:T(8,128)(2,1)} %values.1) | copy-start | bytes 4718596
  13.1 2.0 %copy-start.5 = (bf16[16,2,8192]{2,1,0:T(2,128)(2,1)S(1)}, bf16[16,2,8192]{2,1,0:T(2,128)(2,1)}, u32[]{:S(2)}) copy-start(bf16[16,2,8192]{2,1,0:T(2,128)(2,1)} %param.17) | copy-start | bytes 1572868
  15.3 3.4 %copy-start.36 = (bf16[16,2,2048]{2,1,0:T(2,128)(2,1)S(1)}, bf16[16,2,2048]{2,1,0:T(2,128)(2,1)}, u32[]{:S(2)}) copy-start(bf16[16,2,2048]{2,1,0:T(2,128)(2,1)} %param.18) | copy-start | bytes 393220
  15.3 3.5 %copy-start.3 = (bf16[64,64,256]{2,1,0:T(8,128)(2,1)S(1)}, bf16[64,64,256]{2,1,0:T(8,128)(2,1)}, u32[]{:S(2)}) copy-start(bf16[64,64,256]{2,1,0:T(8,128)(2,1)} %gather_fusion.1) | copy-start | bytes 6291460
  21.2 3.8 %copy-start.4 = (bf16[8192,256]{1,0:T(8,128)(2,1)S(1)}, bf16[8192,256]{1,0:T(8,128)(2,1)}, u32[]{:S(2)}) copy-start(bf16[8192,256]{1,0:T(8,128)(2,1)} %param.25) | copy-start | bytes 12582916
  21.2 3.8 %copy-start.6 = (bf16[16,2,8192]{2,1,0:T(2,128)(2,1)S(1)}, bf16[16,2,8192]{2,1,0:T(2,128)(2,1)}, u32[]{:S(2)}) copy-start(bf16[16,2,8192]{2,1,0:T(2,128)(2,1)} %param.17) | copy-start | bytes 1572868
  25.0 1.6 %copy-start.2 = (bf16[64,64,256]{2,1,0:T(8,128)(2,1)S(1)}, bf16[64,64,256]{2,1,0:T(8,128)(2,1)}, u32[]{:S(2)}) copy-start(bf16[64,64,256]{2,1,0:T(8,128)(2,1)} %gather_fusion) | copy-start | bytes 6291460
  26.6 2.0 %copy-start.40 = (s32[4]{0:T(128)S(1)}, s32[4]{0:T(128)}, u32[]{:S(2)}) copy-start(s32[4]{0:T(128)} %constant.96.clone) | copy-start | bytes 52
  31.0 3.8 %collective-permute-start.69 = (s32[2,2,16]{2,0,1:T(2,128)S(1)}, s32[2,2,16]{2,0,1:T(2,128)S(1)}, u32[]{:S(2)}, u32[]{:S(2)}) collective-permute-start(s32[2,2,16]{2,0,1:T(2,128)S(1)} %pad_add_fusion.1), channel_id=1, source_target_pairs={{0,4},{4,0},{8,12},{12,8},{1,5},{5,1},{9,13},{13,9},{2,6},{6,2},{1... | collective-permute-start | bytes 776 | tf_op jit(solution)/shard_map/ppermute | solution.py:422
  38.9 3.5 %collective-permute-start.70 = (s32[2]{0:T(128)S(1)}, s32[2]{0:T(128)S(1)}, u32[]{:S(2)}, u32[]{:S(2)}) collective-permute-start(s32[2]{0:T(128)S(1)} %pad_add_fusion.3), channel_id=1, source_target_pairs={{0,16},{16,0},{1,17},{17,1},{2,18},{18,2},{3,19},{19,3},{4,20},{20... | collective-permute-start | bytes 32 | tf_op jit(solution)/shard_map/ppermute | solution.py:436
  66.1 22.0 %collective-permute-start.11 = (bf16[2,1152,256]{2,1,0:T(8,128)(2,1)}, bf16[2,1152,256]{2,1,0:T(8,128)(2,1)S(1)}, u32[]{:S(2)}, u32[]{:S(2)}) collective-permute-start(bf16[2,1152,256]{2,1,0:T(8,128)(2,1)} %get-tuple-element.94.refs_0_), channel_id=1, source_target_pairs={{0,4},{1,5},{4,0},{5,1},{8,12},{9,13},{12,8},{13,9},{16,20},{17,21... | collective-permute-start | bytes 3538952 | tf_op jit(solution)/shard_map/cond/branch_1_fun/ppermute | solution.py:393
  68.0 30.5 %collective-permute-start.9 = (bf16[2,1152,256]{2,1,0:T(8,128)(2,1)}, bf16[2,1152,256]{2,1,0:T(8,128)(2,1)S(1)}, u32[]{:S(2)}, u32[]{:S(2)}) collective-permute-start(bf16[2,1152,256]{2,1,0:T(8,128)(2,1)} %get-tuple-element.94.refs_0_), channel_id=1, source_target_pairs={{0,8},{1,9},{4,12},{5,13},{8,0},{9,1},{12,4},{13,5},{16,24},{17,25... | collective-permute-start | bytes 3538952 | tf_op jit(solution)/shard_map/cond/branch_1_fun/ppermute | solution.py:393
  70.4 2.1 %copy-start.9 = (bf16[16,2,2048]{2,1,0:T(2,128)(2,1)}, bf16[16,2,2048]{2,1,0:T(2,128)(2,1)S(1)}, u32[]{:S(2)}) copy-start(bf16[16,2,2048]{2,1,0:T(2,128)(2,1)S(1)} %copy.99.refs_0_) | copy-start | bytes 393220 | tf_op jit(solution)/shard_map/cond
  70.4 1.4 %collective-permute-start.12 = (bf16[16,2,2048]{2,1,0:T(2,128)(2,1)S(1)}, bf16[16,2,2048]{2,1,0:T(2,128)(2,1)S(1)}, u32[]{:S(2)}, u32[]{:S(2)}) collective-permute-start(bf16[16,2,2048]{2,1,0:T(2,128)(2,1)S(1)} %copy.99.refs_0_), channel_id=1, source_target_pairs={{2,10},{3,11},{6,14},{7,15},{10,2},{11,3},{14,6},{15,7},{18,26},{1... | collective-permute-start | bytes 393224 | tf_op jit(solution)/shard_map/cond/branch_1_fun/ppermute | solution.py:393
  71.1 1.4 %collective-permute-start.13 = (bf16[16,2,2048]{2,1,0:T(2,128)(2,1)S(1)}, bf16[16,2,2048]{2,1,0:T(2,128)(2,1)S(1)}, u32[]{:S(2)}, u32[]{:S(2)}) collective-permute-start(bf16[16,2,2048]{2,1,0:T(2,128)(2,1)S(1)} %copy.99.refs_0_), channel_id=1, source_target_pairs={{2,6},{3,7},{6,2},{7,3},{10,14},{11,15},{14,10},{15,11},{18,22},{1... | collective-permute-start | bytes 393224 | tf_op jit(solution)/shard_map/cond/branch_1_fun/ppermute | solution.py:393
  71.7 0.7 copy-start.18
  71.7 0.7 collective-permute-start.14
  72.4 0.6 copy-start.24
  72.5 0.7 copy-start.31
  75.8 12.0 %collective-permute-start.15 = (bf16[24,2,2048]{2,1,0:T(2,128)(2,1)}, bf16[24,2,2048]{2,1,0:T(2,128)(2,1)S(1)}, u32[]{:S(2)}, u32[]{:S(2)}) collective-permute-start(bf16[24,2,2048]{2,1,0:T(2,128)(2,1)} %place.8), channel_id=1, source_target_pairs={{2,0},{3,1},{6,4},{7,5},{10,8},{11,9},{14,12},{15,13},{18,16},{19,... | collective-permute-start | bytes 589832 | tf_op jit(solution)/shard_map/cond/branch_1_fun/ppermute | solution.py:385
  77.1 18.7 %collective-permute-start.10 = (bf16[2,384,256]{2,1,0:T(8,128)(2,1)}, bf16[2,384,256]{2,1,0:T(8,128)(2,1)S(1)}, u32[]{:S(2)}, u32[]{:S(2)}) collective-permute-start(bf16[2,384,256]{2,1,0:T(8,128)(2,1)} %get-tuple-element.95), channel_id=1, source_target_pairs={{2,0},{3,1},{6,4},{7,5},{10,8},{11,9},{14,12},{15,13},{18,16},{19,... | collective-permute-start | bytes 1179656 | tf_op jit(solution)/shard_map/cond/branch_1_fun/ppermute | solution.py:385
  98.5 6.7 %collective-permute-start.16 = (bf16[2,1152,256]{2,1,0:T(8,128)(2,1)S(1)}, bf16[2,1152,256]{2,1,0:T(8,128)(2,1)S(1)}, u32[]{:S(2)}, u32[]{:S(2)}) collective-permute-start(bf16[2,1152,256]{2,1,0:T(8,128)(2,1)S(1)} %collective-permute-done.9.refs_0_), channel_id=1, source_target_pairs={{0,4},{1,5},{4,0},{5,1},{8,12},{9,13},{12,8},{13,9},{16,20},{17,21... | collective-permute-start | bytes 3538952 | tf_op jit(solution)/shard_map/cond/branch_1_fun/ppermute | solution.py:393
  100.4 4.7 %collective-permute-start.17 = (bf16[2,384,256]{2,1,0:T(8,128)(2,1)S(1)}, bf16[2,384,256]{2,1,0:T(8,128)(2,1)S(1)}, u32[]{:S(2)}, u32[]{:S(2)}) collective-permute-start(bf16[2,384,256]{2,1,0:T(8,128)(2,1)S(1)} %collective-permute-done.10.refs_1_), channel_id=1, source_target_pairs={{0,4},{1,5},{4,0},{5,1},{8,12},{9,13},{12,8},{13,9},{16,20},{17,21... | collective-permute-start | bytes 1179656 | tf_op jit(solution)/shard_map/cond/branch_1_fun/ppermute | solution.py:393
  107.3 0.7 copy-start.14
